TPU v7x, 512 devices: a whole 4x4x16 slice. The times are simulated.
512 devices in a mesh: dp: 16 (over x, y), mp: 32 (over z, core).
Axes of the slice: x: 4, y: 4, z: 16, core: 2. Of those that a mesh axis runs over, the one named last changes fastest.
Arguments:
- gradients: bfloat16 [16, 32, 7168, 128], P('dp', None, 'mp'), may hold values from -6 to 6
- owners: int32 [32], replicated, may hold values from 0 to 31, as said below
- momentum: bfloat16 [64, 32, 224, 128], P('mp', None, 'dp'), may hold values from -8 to 8
- master: float32 [64, 32, 224, 128], P('mp', None, 'dp'), may hold values from -0.06 to 0.06
Outputs:
- weights: bfloat16 [32, 7168, 128], P(None, 'mp')
- scales: float32 [32], replicated
- new_momentum: bfloat16 [64, 32, 224, 128], P('mp', None, 'dp')
- new_master: float32 [64, 32, 224, 128], P('mp', None, 'dp')
Inputs may be any that keep to these rules, and one draw needn't show every extreme that they name: `owners`: no index of mp owns more than 2 blocks, and one owns exactly 2.
All inputs are finite; a program needn't handle non-finite values.
Results may differ from a plain program's by a relative error of at most 0.009.
Values may be sent and summed in bfloat16 or wider, within the bound.
A program may use at most 64 MiB of HBM per device.

v0:
```python
import math

import jax
import jax.numpy as jnp
from jax import lax
from jax.sharding import PartitionSpec as P

D = 7168
ITERS = 5


NEWTON = (3.4445, -4.775, 2.0315)
decay_rate = 0.95
learn_rate = 0.05
weight_decay = 0.1
update_gain = 0.2


def as_sent(x):

    def short(part):
        return part.astype(jnp.bfloat16) if part.dtype == jnp.float32 else part

    return jax.tree.map(short, x)


def slot_table(owners):
    number = owners.shape[0]
    same_owner = owners[:, None] == owners[None, :]
    earlier = jnp.arange(number)[None, :] < jnp.arange(number)[:, None]
    return jnp.sum(jnp.where(same_owner & earlier, 1, 0), axis=1).astype(jnp.int32)


def gram_total(values):
    local_gram = jnp.einsum("srh,srk->shk", values, values, precision=lax.Precision.HIGHEST)
    return lax.psum(local_gram, "dp")


def body(gradients, owners, momentum, master):
    capacity = momentum.shape[0]
    groups = lax.axis_size("mp")
    piece_rows = momentum.shape[2]
    head_size = momentum.shape[3]
    blocks_all = owners.shape[0]
    reduced = lax.psum_scatter(
        gradients[0].astype(jnp.float32), "dp", scatter_dimension=1, tiled=True
    )
    position = slot_table(owners)
    slot_ids = owners * capacity + position
    targets = (jnp.arange(groups)[None, :] * capacity + jnp.arange(capacity)[:, None]).reshape(-1)
    matches = slot_ids[None, :] == targets[:, None]
    present = jnp.any(matches, axis=1)
    chosen = jnp.sum(jnp.where(matches, jnp.arange(blocks_all)[None, :], 0), axis=1)
    outgoing = jnp.where(present[:, None, None], reduced[chosen], 0.0)
    outgoing = outgoing.reshape(capacity, groups, piece_rows, head_size)
    arrived = lax.all_to_all(outgoing, "mp", split_axis=1, concat_axis=1, tiled=True)
    own_index = lax.axis_index("mp")
    own_slots = own_index * capacity + jnp.arange(capacity)
    occupied = jnp.any(slot_ids[None, :] == own_slots[:, None], axis=1)
    momentum_new = (decay_rate * momentum.astype(jnp.float32) + arrived).astype(jnp.bfloat16)
    update = (arrived + decay_rate * momentum_new.astype(jnp.float32)).reshape(
        capacity, -1, head_size
    )
    raw_gram = gram_total(update)
    squares = jnp.trace(raw_gram, axis1=1, axis2=2)
    norm_value = jnp.sqrt(squares) + 1e-07
    current = update / norm_value[:, None, None]
    gram_now = raw_gram / (norm_value * norm_value)[:, None, None]
    for iteration in range(ITERS):
        if iteration > 0:
            gram_now = gram_total(current)
        mixing = NEWTON[1] * gram_now + NEWTON[2] * jnp.einsum(
            "shk,skl->shl", gram_now, gram_now, precision=lax.Precision.HIGHEST
        )
        current = NEWTON[0] * current + jnp.einsum(
            "srh,shk->srk", current, mixing, precision=lax.Precision.HIGHEST
        )
    weight_rows = master.reshape(capacity, -1, head_size)
    updated = (
        weight_rows * (1.0 - learn_rate * weight_decay)
        - learn_rate * update_gain * math.sqrt(D) * current
    )
    peak_value = lax.pmax(jnp.max(jnp.abs(updated), axis=(1, 2)), "dp") + 1e-06
    quantized = (updated / peak_value[:, None, None]).astype(jnp.bfloat16)
    quantized = quantized.reshape(capacity, groups, piece_rows, head_size)
    new_momentum = jnp.where(occupied[:, None, None, None], momentum_new, momentum)
    new_master = jnp.where(occupied[:, None, None, None], updated.reshape(master.shape), master)
    peak_copies = jnp.broadcast_to(peak_value[:, None, None], (capacity, groups, 1))
    pick_order = position * groups + owners
    gathered = lax.all_gather(quantized, "dp", axis=2, tiled=True)
    returned, peak_back = (
        lax.all_to_all(gathered, "mp", split_axis=1, concat_axis=1, tiled=True),
        lax.all_to_all(as_sent(peak_copies), "mp", split_axis=1, concat_axis=1, tiled=True).astype(
            peak_copies.dtype
        ),
    )
    weights = returned.reshape(capacity * groups, -1, head_size)[pick_order]
    scales = peak_back.reshape(-1)[pick_order]
    return (weights, scales, new_momentum, new_master)


def solution(mesh):
    in_specs = (
        P("dp", None, "mp", None),
        P(),
        P("mp", None, "dp", None),
        P("mp", None, "dp", None),
    )
    out_specs = (P(None, "mp", None), P(), P("mp", None, "dp", None), P("mp", None, "dp", None))
    return jax.shard_map(body, mesh=mesh, in_specs=in_specs, out_specs=out_specs, check_vma=False)
```

profile of v0, /device:TPU:1, one launch (start us, length us, event | category | flops | bytes accessed | tf_op | source)
XLA Modules:
  0.0 1025.4 jit_solution(6841690551971895699)
XLA Ops:
  7.2 0.0 reduce-scatter.2.cloned.1.call-start
  7.2 3.9 bitcast_convert_fusion
  11.1 0.0 reduce-scatter.2.cloned.1.call-update
  11.1 0.0 all-reduce.6.cloned.1.call-start
  11.2 0.1 add.118
  11.3 0.5 copy-done.2
  11.8 0.2 select_reduce_fusion.1
  11.9 0.1 compare_reduce_fusion
  12.0 0.1 broadcast_in_dim.86
  12.1 0.1 fusion.14
  12.2 95.5 %reduce-scatter.2.cloned.1.call-done = f32[32,14,128]{2,0,1:T(8,128)} async-done(((f32[32,224,128]{2,0,1:T(8,128)}), f32[32,14,128]{2,0,1:T(8,128)}) %reduce-scatter.2.cloned.1.call-update) | async-done | bytes 229392 | tf_op jit(solution)/shard_map/reduce_scatter | solution.py:45
  107.7 1.1 copy.80
  108.8 0.6 gather_fusion
  109.5 0.2 copy.81
  109.6 0.1 broadcast_select_fusion.1
  109.7 0.4 copy.82
  110.1 45.2 %all_to_all.15 = f32[2,32,14,128]{3,0,2,1:T(2,128)S(1)} all-to-all(f32[2,32,14,128]{3,0,2,1:T(2,128)S(1)} %copy.82), channel_id=1, replica_groups=mesh['dp'=16,'mp'=32] {'mp'}, dimensions={1} | all-to-all | bytes 917504 | tf_op jit(solution)/shard_map/all_to_all | solution.py:56
  155.3 0.5 multiply_add_fusion
  155.8 1.7 fusion.8
  157.5 0.0 all-reduce.6.cloned.1.call-update
  157.5 0.0 all-reduce.8.cloned.1.call-start
  157.6 100.7 %all-reduce.6.cloned.1.call-done = f32[2,128,128]{2,1,0:T(8,128)} async-done(((f32[2,128,128]{2,1,0:T(8,128)}), f32[2,128,128]{2,1,0:T(8,128)}) %all-reduce.6.cloned.1.call-update) | async-done | bytes 131088 | tf_op jit(solution)/shard_map/psum | solution.py:36
  258.3 1.0 select_reduce_fusion
  259.3 1.4 fusion.6
  260.7 0.6 convolution_add_fusion.4
  261.3 1.7 fusion.19
  263.0 0.0 all-reduce.10.cloned.1.call-start
  263.1 112.6 %all-reduce.8.cloned.1.call-done = f32[2,128,128]{2,1,0:T(8,128)} async-done(((f32[2,128,128]{2,1,0:T(8,128)}), f32[2,128,128]{2,1,0:T(8,128)}) %all-reduce.8.cloned.1.call-update) | async-done | bytes 131088 | tf_op jit(solution)/shard_map/psum | solution.py:36
  375.6 1.3 fusion.5
  377.0 0.5 convolution_add_fusion.3
  377.5 1.7 fusion.20
  379.2 0.0 all-reduce.12.cloned.1.call-start
  379.2 112.6 %all-reduce.10.cloned.1.call-done = f32[2,128,128]{2,1,0:T(8,128)} async-done(((f32[2,128,128]{2,1,0:T(8,128)}), f32[2,128,128]{2,1,0:T(8,128)}) %all-reduce.10.cloned.1.call-update) | async-done | bytes 131088 | tf_op jit(solution)/shard_map/psum | solution.py:36
  491.8 1.3 fusion.4
  493.2 0.5 convolution_add_fusion.2
  493.7 1.7 fusion.21
  495.4 0.0 all-reduce.14.cloned.1.call-start
  495.5 112.8 %all-reduce.12.cloned.1.call-done = f32[2,128,128]{2,1,0:T(8,128)} async-done(((f32[2,128,128]{2,1,0:T(8,128)}), f32[2,128,128]{2,1,0:T(8,128)}) %all-reduce.12.cloned.1.call-update) | async-done | bytes 131088 | tf_op jit(solution)/shard_map/psum | solution.py:36
  608.3 1.3 fusion.3
  609.6 0.5 convolution_add_fusion.1
  610.1 1.7 fusion.22
  611.8 0.2 all-gather.2.cloned.1.call-start
  612.1 0.4 copy.78
  612.5 112.0 %all-reduce.14.cloned.1.call-done = f32[2,128,128]{2,1,0:T(8,128)} async-done(((f32[2,128,128]{2,1,0:T(8,128)}), f32[2,128,128]{2,1,0:T(8,128)}) %all-reduce.14.cloned.1.call-update) | async-done | bytes 131088 | tf_op jit(solution)/shard_map/psum | solution.py:36
  724.5 1.3 fusion.2
  725.8 0.7 abs_reduce_fusion
  726.5 31.4 %pmax.7 = f32[2]{0:T(128)S(1)} all-reduce(f32[2]{0:T(128)S(1)} %get-tuple-element.30), channel_id=1, replica_groups=mesh['dp'=16,'mp'=32] {'dp'}, use_global_device_ids=true, to_apply=%region_11.12 | all-reduce | flops 2 | bytes 16 | tf_op jit(solution)/shard_map/pmax | solution.py:83
  757.9 0.1 divide_convert_fusion
  758.0 0.9 copy.88
  759.0 32.8 %all_to_all.16 = bf16[2,32,1]{0,2,1:T(2,128)(2,1)S(1)} all-to-all(bf16[2,32,1]{0,2,1:T(2,128)(2,1)S(1)} %broadcast_in_dim.94), channel_id=1, replica_groups=mesh['dp'=16,'mp'=32] {'mp'}, dimensions={1} | all-to-all | bytes 256 | tf_op jit(solution)/shard_map/all_to_all | solution.py:93
  791.8 42.4 %all-gather.2.cloned.1.call-done = bf16[2,32,224,128]{3,0,2,1:T(2,128)(2,1)} async-done(((bf16[2,32,14,128]{3,0,2,1:T(2,128)(2,1)}), bf16[2,32,224,128]{3,0,2,1:T(2,128)(2,1)}) %all-gather.2.cloned.1.call-update) | async-done | bytes 3670032 | tf_op jit(solution)/shard_map/all_gather | solution.py:90
  834.2 13.9 %all-to-all-start.1 = ((bf16[2,32,224,128]{3,0,2,1:T(2,128)(2,1)}), bf16[2,32,224,128]{3,0,2,1:T(2,128)(2,1)}, u32[]{:S(2)}, u32[]{:S(2)}) async-start(bf16[2,32,224,128]{3,0,2,1:T(2,128)(2,1)} %all-gather.2.cloned.1.call-done), calls=%async_computation.2 | async-start | bytes 7340032 | tf_op jit(solution)/shard_map/all_to_all | solution.py:92
  848.2 0.2 compare_reduce_fusion.1
  848.4 0.5 broadcast_select_fusion
  848.8 0.7 copy.94
  849.6 0.4 copy.92
  849.9 0.5 copy_select_fusion
  850.4 0.8 copy.95
  851.2 0.1 copy.90
  851.3 0.1 reshape.99
  851.4 1.2 gather_fusion.2
  852.6 157.5 %all-to-all-done.1 = bf16[2,32,224,128]{3,0,2,1:T(2,128)(2,1)} async-done(((bf16[2,32,224,128]{3,0,2,1:T(2,128)(2,1)}), bf16[2,32,224,128]{3,0,2,1:T(2,128)(2,1)}, u32[]{:S(2)}, u32[]{:S(2)}) %all-to-all-start.1) | async-done | bytes 3670048 | tf_op jit(solution)/shard_map/all_to_all | solution.py:92
  1010.1 4.4 copy.89
  1014.5 4.0 gather_fusion.1
  (22 shorter events, 0.2 us)
Async XLA Ops:
  7.2 100.6 %reduce-scatter.2.cloned.1.call-start = ((), (), s32[]{:S(2)}) async-start(), calls=%async_computation.4 | async-start | bytes 3899392 | tf_op jit(solution)/shard_map/reduce_scatter | solution.py:45
  11.1 0.7 copy-start.2
  11.1 247.1 %all-reduce.6.cloned.1.call-start = ((), (), s32[]{:S(2)}) async-start(), calls=%async_computation.5 | async-start | bytes 262144 | tf_op jit(solution)/shard_map/psum | solution.py:36
  109.5 45.9 %copy-start.1 = (bf16[2,32,14,128]{3,1,2,0:T(8,128)(2,1)S(1)}, bf16[2,32,14,128]{3,1,2,0:T(8,128)(2,1)}, u32[]{:S(2)}) copy-start(bf16[2,32,14,128]{3,1,2,0:T(8,128)(2,1)} %param.6) | copy-start | bytes 688132
  157.5 218.1 %all-reduce.8.cloned.1.call-start = ((), (), s32[]{:S(2)}) async-start(), calls=%async_computation.6 | async-start | bytes 262144 | tf_op jit(solution)/shard_map/psum | solution.py:36
  263.0 228.8 %all-reduce.10.cloned.1.call-start = ((), (), s32[]{:S(2)}) async-start(), calls=%async_computation.7 | async-start | bytes 262144 | tf_op jit(solution)/shard_map/psum | solution.py:36
  379.2 229.1 %all-reduce.12.cloned.1.call-start = ((), (), s32[]{:S(2)}) async-start(), calls=%async_computation.8 | async-start | bytes 262144 | tf_op jit(solution)/shard_map/psum | solution.py:36
  493.7 118.4 %copy-start = (f32[2,32,14,128]{3,1,2,0:T(8,128)S(1)}, f32[2,32,14,128]{3,1,2,0:T(8,128)}, u32[]{:S(2)}) copy-start(f32[2,32,14,128]{3,1,2,0:T(8,128)} %param.7) | copy-start | bytes 1376260
  495.4 229.1 %all-reduce.14.cloned.1.call-start = ((), (), s32[]{:S(2)}) async-start(), calls=%async_computation.9 | async-start | bytes 262144 | tf_op jit(solution)/shard_map/psum | solution.py:36
  611.8 222.4 %all-gather.2.cloned.1.call-start = ((), (), s32[]{:S(2)}) async-start(), calls=%async_computation.10 | async-start | bytes 3899392 | tf_op jit(solution)/shard_map/all_gather | solution.py:90
  834.2 175.9 %all-to-all-start.1 = ((bf16[2,32,224,128]{3,0,2,1:T(2,128)(2,1)}), bf16[2,32,224,128]{3,0,2,1:T(2,128)(2,1)}, u32[]{:S(2)}, u32[]{:S(2)}) async-start(bf16[2,32,224,128]{3,0,2,1:T(2,128)(2,1)} %all-gather.2.cloned.1.call-done), calls=%async_computation.2 | async-start | bytes 7340032 | tf_op jit(solution)/shard_map/all_to_all | solution.py:92
Sparse Core Ops, SparseCore 0:
  12.2 95.4 reduce-scatter.1
  157.6 100.5 all-reduce.5
  263.1 112.4 all-reduce.7
  379.3 112.4 all-reduce.9
  495.8 112.4 all-reduce.11
  612.0 112.4 all-reduce.13
  759.1 75.0 all-gather.1
where the time goes:
time: 1030 us
  waiting for transfers between devices  846 us (82%)
  blocking collectives  110 us (11%)
  matrix products  17.9 us (2%)
  local copies, waits for them, and re-layouts  15.9 us (2%)
  starting transfers between devices  14.4 us (1%)
  between operations  14.4 us (1%)
    psum x5, waiting for transfers between devices, gram_total(): return lax.psum(local_gram, 'dp')  551 us
    all_to_all x1, waiting for transfers between devices, body(): lax.all_to_all(gathered, 'mp', split_axis=1, concat_axis=1, tiled=True)  157 us
    reduce_scatter x1, waiting for transfers between devices, body(): lax.psum_scatter(gradients[0].astype(jnp.float32), 'dp', scatter_dimensio...  95.5 us
    all_to_all x1, blocking collectives, body(): lax.all_to_all(outgoing, 'mp', split_axis=1, concat_axis=1, tiled=True)  45.2 us
    all_gather x1, waiting for transfers between devices, body(): gathered = lax.all_gather(quantized, 'dp', axis=2, tiled=True)  42.4 us
    all_to_all x1, blocking collectives, body(): lax.all_to_all(as_sent(peak_copies), 'mp', split_axis=1, concat_axis=1, t...  32.8 us
    pmax x1, blocking collectives, body(): peak_value = lax.pmax(jnp.max(jnp.abs(updated), axis=(1, 2)), 'dp') + 1e-06  31.4 us
  transfers between devices with their start and end apart: 8, of which 8 were waited for; matrix products, arithmetic and copies ran while one was open for 1% of the time, Pallas kernels for 0%

commit v1 on v0

v1 whole, which is shorter than its diff:
```python
import functools
import math

import jax
import jax.numpy as jnp
from jax import lax
from jax.experimental import pallas as pl
from jax.experimental.pallas import tpu as pltpu
from jax.sharding import PartitionSpec as P

D = 7168
ITERS = 5
NEWTON = (3.4445, -4.775, 2.0315)
decay_rate = 0.95
learn_rate = 0.05
weight_decay = 0.1
update_gain = 0.2

MESH = pl.DeviceIdType.MESH
F32 = jnp.float32
BF16 = jnp.bfloat16
PAD = 16


def dot(a, b):
    return jnp.dot(a, b, precision=lax.Precision.HIGHEST, preferred_element_type=F32)


def kernel(n_dp, n_mp, cap, blocks, rows, owners_ref, grad_ref, mom_ref, master_ref,
           out_ref, scale_ref, newmom_ref, newmaster_ref,
           wide, rs_out, rs_in, z32, z_out, z_in, upd, gram_out, gram_in, gram_all,
           y_out, y_in, ag_out, ag_in,
           rs_s, rs_r, z_s, z_r, g_s, g_r, h_s, h_r, y_s, y_r, ag_s, ag_r):
    dp, mp = lax.axis_index("dp"), lax.axis_index("mp")
    slots = n_mp * cap
    shard = n_dp * rows
    msg = cap * PAD

    def dp_peer(k):
        return lax.rem(dp + k, n_dp), lax.rem(dp + n_dp - k, n_dp)

    def mp_peer(k):
        return lax.rem(mp + k, n_mp), lax.rem(mp + n_mp - k, n_mp)

    barrier = pltpu.get_barrier_semaphore()

    @pl.loop(1, n_dp)
    def _(k):
        pl.semaphore_signal(barrier, 1, device_id={"dp": dp_peer(k)[0]}, device_id_type=MESH)

    @pl.loop(1, n_mp)
    def _(k):
        pl.semaphore_signal(barrier, 1, device_id={"mp": mp_peer(k)[0]}, device_id_type=MESH)

    @pl.loop(0, blocks)
    def _(b):
        at = pl.ds(pl.multiple_of(b * shard, 16), shard)
        wide[at, :] = grad_ref[at, :].astype(F32)

    def pick(d):
        for r in range(rows):
            x = wide[pl.ds(d * rows + r, blocks, stride=shard), :]
            rs_out[d, r] = x.astype(BF16)

    lane = lax.broadcasted_iota(jnp.int32, (8, 128), 1)
    owner_row = jnp.full((8, 128), -1, jnp.int32)
    for b in range(blocks):
        owner_row = jnp.where(lane == b, owners_ref[b], owner_row)
    position = jnp.zeros((8, 128), jnp.int32)
    for b in range(blocks):
        position = position + jnp.where((owner_row == owners_ref[b]) & (lane > b), 1, 0)
    slot_row = jnp.where(owner_row >= 0, owner_row * cap + position, -1)[0:1, 0:blocks]
    place = jnp.broadcast_to(slot_row, (slots, blocks)) == lax.broadcasted_iota(jnp.int32, (slots, blocks), 0)
    onehot = jnp.where(place, 1.0, 0.0).astype(F32)
    onehot_t = onehot.T.astype(BF16)
    onehot = onehot.astype(BF16)
    count = jnp.int32(0)
    for b in range(blocks):
        count = count + jnp.where(owners_ref[b] == mp, 1, 0)

    pl.semaphore_wait(barrier, n_dp + n_mp - 2)

    def rs_copy(k):
        to, _ = dp_peer(k)
        return pltpu.make_async_remote_copy(
            src_ref=rs_out.at[to], dst_ref=rs_in.at[dp], send_sem=rs_s.at[k], recv_sem=rs_r.at[k],
            device_id={"dp": to}, device_id_type=MESH)

    @pl.loop(1, n_dp)
    def _(k):
        pick(dp_peer(k)[0])
        rs_copy(k).start()

    pick(dp)
    rs_in[dp] = rs_out[dp]

    z32[...] = jnp.zeros_like(z32)

    @pl.loop(1, n_dp)
    def _(k):
        _, source = dp_peer(k)
        pltpu.make_async_remote_copy(
            src_ref=rs_out.at[dp], dst_ref=rs_in.at[source], send_sem=rs_s.at[k], recv_sem=rs_r.at[k],
            device_id={"dp": source}, device_id_type=MESH).wait_recv()

    for r in range(rows):
        total = rs_in[0, r].astype(F32)
        for s in range(1, n_dp):
            total = total + rs_in[s, r].astype(F32)
        z32[pl.ds(r, slots, stride=PAD), :] = jnp.dot(onehot, total.astype(BF16), preferred_element_type=F32)

    z_out[...] = z32[...].astype(BF16).reshape(z_out.shape)

    def z_copy(k, src, dst, s, r):
        to, _ = mp_peer(k)
        return pltpu.make_async_remote_copy(
            src_ref=src.at[to], dst_ref=dst.at[mp], send_sem=s.at[k], recv_sem=r.at[k],
            device_id={"mp": to}, device_id_type=MESH)

    def z_wait(k, src, dst, s, r):
        _, source = mp_peer(k)
        pltpu.make_async_remote_copy(
            src_ref=src.at[mp], dst_ref=dst.at[source], send_sem=s.at[k], recv_sem=r.at[k],
            device_id={"mp": source}, device_id_type=MESH).wait_recv()

    @pl.loop(1, n_mp)
    def _(k):
        z_copy(k, z_out, z_in, z_s, z_r).start()

    z_in[mp] = z_out[mp]

    @pl.loop(1, n_mp)
    def _(k):
        z_wait(k, z_out, z_in, z_s, z_r)

    z32[...] = z_in[...].reshape(z32.shape).astype(F32)
    held = n_mp * rows
    for c in range(cap):
        for r in range(rows):
            arrived = z32[pl.ds(c * PAD + r, n_mp, stride=msg), :]
            before = mom_ref[c, r]
            after = (decay_rate * before.astype(F32) + arrived).astype(BF16)
            newmom_ref[c, r] = jnp.where(count > c, after, before)
            upd[c, pl.ds(r * n_mp, n_mp), :] = arrived + decay_rate * after.astype(F32)

    piece = 128 // n_dp
    for c in range(cap):
        u = upd[c]
        gram = lax.dot_general(u, u, (((0,), (0,)), ((), ())), precision=lax.Precision.HIGHEST,
                               preferred_element_type=F32)
        for d in range(n_dp):
            gram_out[d, c] = gram[d * piece:(d + 1) * piece, :]

    @pl.loop(1, n_dp)
    def _(k):
        to, _ = dp_peer(k)
        pltpu.make_async_remote_copy(
            src_ref=gram_out.at[to], dst_ref=gram_in.at[dp], send_sem=g_s.at[k], recv_sem=g_r.at[k],
            device_id={"dp": to}, device_id_type=MESH).start()

    gram_in[dp] = gram_out[dp]

    @pl.loop(1, n_dp)
    def _(k):
        _, source = dp_peer(k)
        pltpu.make_async_remote_copy(
            src_ref=gram_out.at[dp], dst_ref=gram_in.at[source], send_sem=g_s.at[k], recv_sem=g_r.at[k],
            device_id={"dp": source}, device_id_type=MESH).wait_recv()

    part = gram_in[0]
    for s in range(1, n_dp):
        part = part + gram_in[s]
    gram_all[dp] = part

    @pl.loop(1, n_dp)
    def _(k):
        to, _ = dp_peer(k)
        pltpu.make_async_remote_copy(
            src_ref=gram_all.at[dp], dst_ref=gram_all.at[dp], send_sem=h_s.at[k], recv_sem=h_r.at[k],
            device_id={"dp": to}, device_id_type=MESH).start()

    @pl.loop(1, n_dp)
    def _(k):
        _, source = dp_peer(k)
        pltpu.make_async_remote_copy(
            src_ref=gram_all.at[dp], dst_ref=gram_all.at[source], send_sem=h_s.at[k], recv_sem=h_r.at[k],
            device_id={"dp": source}, device_id_type=MESH).wait_recv()

    eye = lax.broadcasted_iota(jnp.int32, (128, 128), 0) == lax.broadcasted_iota(jnp.int32, (128, 128), 1)
    a0, a1, a2 = NEWTON
    grams, polys, norms = [], [], []
    for c in range(cap):
        raw = gram_all[:, c].reshape(128, 128)
        norm = jnp.sqrt(jnp.sum(jnp.where(eye, raw, 0.0), axis=(0, 1), keepdims=True)) + 1e-07
        grams.append(raw / (norm * norm))
        norms.append(norm)
    polys = [None] * cap
    for i in range(ITERS):
        mixes = [a1 * g + a2 * dot(g, g) for g in grams]
        if i == 0:
            polys = [jnp.where(eye, a0, 0.0) + m for m in mixes]
        else:
            polys = [a0 * p + dot(p, m) for p, m in zip(polys, mixes)]
        if i < ITERS - 1:
            halves = [a0 * g + dot(m, g) for g, m in zip(grams, mixes)]
            grams = [a0 * h + dot(h, m) for h, m in zip(halves, mixes)]

    for c in range(cap):
        step = dot(upd[c], polys[c] * (-learn_rate * update_gain * math.sqrt(D) / norms[c]))
        peak = jnp.zeros((n_mp, 128), F32)
        for r in range(rows):
            before = master_ref[c, r]
            after = before * (1.0 - learn_rate * weight_decay) + step[r * n_mp:(r + 1) * n_mp, :]
            newmaster_ref[c, r] = jnp.where(count > c, after, before)
            peak = jnp.maximum(peak, jnp.abs(after))
            z32[pl.ds(c * PAD + r, n_mp, stride=msg), :] = after
        peak = jnp.broadcast_to(jnp.max(peak, axis=(0, 1), keepdims=True), (n_mp, 128))
        high = peak.astype(BF16).astype(F32)
        low = peak - high
        first = lax.broadcasted_iota(jnp.int32, (n_mp, 128), 1) < 64
        z32[pl.ds(c * PAD + rows, n_mp, stride=msg), :] = jnp.where(first, high, low)

    y_out[...] = z32[...].astype(BF16).reshape(y_out.shape)

    @pl.loop(1, n_mp)
    def _(k):
        z_copy(k, y_out, y_in, y_s, y_r).start()

    y_in[mp] = y_out[mp]

    @pl.loop(1, n_mp)
    def _(k):
        z_wait(k, y_out, y_in, y_s, y_r)

    z32[...] = y_in[...].reshape(z32.shape).astype(F32)
    for r in range(rows + 1):
        x = z32[pl.ds(r, slots, stride=PAD), :].astype(BF16)
        ag_out[r] = jnp.dot(onehot_t, x, preferred_element_type=F32).astype(BF16)

    @pl.loop(1, n_dp)
    def _(k):
        to, _ = dp_peer(k)
        pltpu.make_async_remote_copy(
            src_ref=ag_out, dst_ref=ag_in.at[dp], send_sem=ag_s.at[k], recv_sem=ag_r.at[k],
            device_id={"dp": to}, device_id_type=MESH).start()

    ag_in[dp] = ag_out[...]

    def spread(source):
        for r in range(rows):
            wide[pl.ds(source * rows + r, blocks, stride=shard), :] = ag_in[source, r].astype(F32)

    spread(dp)

    @pl.loop(1, n_dp)
    def _(k):
        _, source = dp_peer(k)
        pltpu.make_async_remote_copy(
            src_ref=ag_out, dst_ref=ag_in.at[source], send_sem=ag_s.at[k], recv_sem=ag_r.at[k],
            device_id={"dp": source}, device_id_type=MESH).wait_recv()
        spread(source)

    both = [ag_in[s, rows].astype(F32) for s in range(n_dp)]
    peaks = [x + pltpu.roll(x, 64, 1) for x in both]
    peak = functools.reduce(jnp.maximum, peaks) + 1e-06
    z32[0:blocks, :] = 1.0 / peak
    scale_ref[...] = peak

    @pl.loop(0, blocks)
    def _(b):
        at = pl.ds(pl.multiple_of(b * shard, 16), shard)
        out_ref[at, :] = (wide[at, :] * z32[pl.ds(b, 1), :]).astype(BF16)

    @pl.loop(1, n_dp)
    def _(k):
        rs_copy(k).wait_send()
        for src, s in ((gram_out.at[dp], g_s), (gram_all.at[dp], h_s), (ag_out, ag_s)):
            pltpu.make_async_remote_copy(
                src_ref=src, dst_ref=src, send_sem=s.at[k], recv_sem=s.at[k],
                device_id={"dp": dp_peer(k)[0]}, device_id_type=MESH).wait_send()

    @pl.loop(1, n_mp)
    def _(k):
        z_copy(k, z_out, z_in, z_s, z_r).wait_send()
        z_copy(k, y_out, y_in, y_s, y_r).wait_send()


def body(gradients, owners, momentum, master):
    n_dp, n_mp = lax.axis_size("dp"), lax.axis_size("mp")
    _, blocks, shard, head = gradients.shape
    cap, _, rows, _ = momentum.shape
    slots = n_mp * cap
    msg = cap * PAD
    moved = (cap, rows, n_mp, head)
    sem = pltpu.SemaphoreType.DMA
    vmem = pl.BlockSpec(memory_space=pltpu.VMEM)
    out, scale, newmom, newmaster = pl.pallas_call(
        functools.partial(kernel, n_dp, n_mp, cap, blocks, rows),
        out_shape=(
            jax.ShapeDtypeStruct((blocks * shard, head), BF16),
            jax.ShapeDtypeStruct((blocks, head), F32),
            jax.ShapeDtypeStruct(moved, BF16),
            jax.ShapeDtypeStruct(moved, F32),
        ),
        in_specs=[pl.BlockSpec(memory_space=pltpu.SMEM), vmem, vmem, vmem],
        out_specs=(vmem,) * 4,
        scratch_shapes=[
            pltpu.VMEM((blocks * shard, head), F32),
            pltpu.VMEM((n_dp, rows, blocks, head), BF16),
            pltpu.VMEM((n_dp, rows, blocks, head), BF16),
            pltpu.VMEM((slots * PAD, head), F32),
            pltpu.VMEM((n_mp, msg, head), BF16),
            pltpu.VMEM((n_mp, msg, head), BF16),
            pltpu.VMEM((cap, rows * n_mp, head), F32),
            pltpu.VMEM((n_dp, cap, head // n_dp, head), F32),
            pltpu.VMEM((n_dp, cap, head // n_dp, head), F32),
            pltpu.VMEM((n_dp, cap, head // n_dp, head), F32),
            pltpu.VMEM((n_mp, msg, head), BF16),
            pltpu.VMEM((n_mp, msg, head), BF16),
            pltpu.VMEM((rows + 1, blocks, head), BF16),
            pltpu.VMEM((n_dp, rows + 1, blocks, head), BF16),
            sem((n_dp,)), sem((n_dp,)), sem((n_mp,)), sem((n_mp,)), sem((n_dp,)), sem((n_dp,)),
            sem((n_dp,)), sem((n_dp,)), sem((n_mp,)), sem((n_mp,)), sem((n_dp,)), sem((n_dp,)),
        ],
        compiler_params=pltpu.CompilerParams(
            collective_id=0, has_side_effects=True, vmem_limit_bytes=48 * 2**20),
        name="muon_step",
    )(
        owners,
        gradients.reshape(blocks * shard, head),
        momentum.transpose(0, 2, 1, 3),
        master.transpose(0, 2, 1, 3),
    )
    return (
        out.reshape(blocks, shard, head),
        scale[:, 0],
        newmom.transpose(0, 2, 1, 3),
        newmaster.transpose(0, 2, 1, 3),
    )


def solution(mesh):
    in_specs = (
        P("dp", None, "mp", None),
        P(),
        P("mp", None, "dp", None),
        P("mp", None, "dp", None),
    )
    out_specs = (P(None, "mp", None), P(), P("mp", None, "dp", None), P("mp", None, "dp", None))
    return jax.shard_map(body, mesh=mesh, in_specs=in_specs, out_specs=out_specs, check_vma=False)
```

time: 1030 us -> 145 us (0.14)
  the two profiles are of different devices: /device:TPU:1 before, /device:TPU:28 now
where the time goes in v1:
time: 145 us
  Pallas kernels  137 us (94%)
  local copies, waits for them, and re-layouts  7.41 us (5%)
    pallas_call x1, Pallas kernels, body(): pl.pallas_call(functools.partial(kernel, n_dp, n_mp, cap, blocks, rows),...  137 us
    unnamed x11, local copies, waits for them, and re-layouts  6.79 us

profile of v1, /device:TPU:28, one launch (start us, length us, event | category | flops | bytes accessed | tf_op | source)
XLA Modules:
  0.0 144.9 jit_solution(7282975464670982289)
XLA Ops:
  0.6 0.0 copy-start
  0.6 1.5 %copy-done = bf16[1,32,224,128]{3,2,1,0:T(8,128)(2,1)S(1)} copy-done((bf16[1,32,224,128]{3,2,1,0:T(8,128)(2,1)S(1)}, bf16[1,32,224,128]{3,2,1,0:T(8,128)(2,1)}, u32[]{:S(2)}) %copy-start) | copy-done | bytes 1835032
  2.1 0.0 copy-start.1
  2.1 1.0 copy-done.1
  3.2 0.0 copy-start.2
  3.2 0.9 copy-done.2
  4.1 0.0 copy-start.3
  4.1 0.7 copy-done.3
  4.7 136.8 %muon_step.1 = (bf16[7168,128]{1,0:T(8,128)(2,1)S(1)}, f32[32,128]{1,0:T(8,128)S(1)}, bf16[2,14,32,128]{3,2,1,0:T(8,128)(2,1)S(1)}, f32[2,14,32,128]{3,2,1,0:T(8,128)S(1)}) custom-call(s32[32]{0:T(128)S(1)} %copy-done.3, bf16[7168,128]{1,0:T(8,128)(2,1)S(1)} %bitcast.7, bf16[2,14,32,128]{3,2,1,0:T(8,128)(2,1)S(1)} %bitcast.11, f32[2,14,32,128]{3,2,1,0:T(8,128)S(1)} %bitcast.9), custom_call_target="tpu_custom_call" | custom-call | tf_op jit(solution)/shard_map/muon_step/pallas_call | solution.py:297
  141.6 0.6 slice_reduce_fusion
  142.2 1.2 copy.11
  143.4 0.7 copy.12
  144.1 0.8 copy.13
Async XLA Ops:
  0.6 1.5 %copy-start = (bf16[1,32,224,128]{3,2,1,0:T(8,128)(2,1)S(1)}, bf16[1,32,224,128]{3,2,1,0:T(8,128)(2,1)}, u32[]{:S(2)}) copy-start(bf16[1,32,224,128]{3,2,1,0:T(8,128)(2,1)} %param.4) | copy-start | bytes 5505028
  2.1 1.0 copy-start.1
  3.2 0.9 copy-start.2
  4.1 0.7 copy-start.3

commit v2 on v1

v2 whole, which is shorter than its diff:
```python
import functools
import math

import jax
import jax.numpy as jnp
from jax import lax
from jax.experimental import pallas as pl
from jax.experimental.pallas import tpu as pltpu
from jax.sharding import PartitionSpec as P

D = 7168
ITERS = 5
NEWTON = (3.4445, -4.775, 2.0315)
decay_rate = 0.95
learn_rate = 0.05
weight_decay = 0.1
update_gain = 0.2

MESH = pl.DeviceIdType.MESH
F32 = jnp.float32
BF16 = jnp.bfloat16
SIDE = 4


def dot(a, b):
    return jnp.dot(a, b, precision=lax.Precision.HIGHEST, preferred_element_type=F32)


def kernel(n_dp, n_mp, cap, blocks, rows, owners_hbm, grad_hbm, mom_hbm, master_hbm,
           out_ref, scale_ref, newmom_ref, newmaster_ref,
           owners_ref, grad_ref, mom_ref, master_ref, wide,
           rs1_out_a, rs1_out_b, rs1_in_a, rs1_in_b, rs2_out_a, rs2_out_b, rs2_in_a, rs2_in_b,
           z32, z_out, z_in, upd, gram_out, gram_in, gram_all, y_out, y_in, ag_a, ag_b,
           in_sem, rs1_s, rs1_r, rs2_s, rs2_r, z_s, z_r, g_s, g_r, h_s, h_r, y_s, y_r,
           ag1_s, ag1_r, ag2_s, ag2_r):
    dp, mp = lax.axis_index("dp"), lax.axis_index("mp")
    side = SIDE
    x, y = dp // side, lax.rem(dp, side)
    slots = n_mp * cap
    shard = n_dp * rows
    half = blocks // 2
    few, many = 0, 1
    starts, counts = (8, 0), (rows - 8, 8)
    rs1_out, rs1_in = (rs1_out_a, rs1_out_b), (rs1_in_a, rs1_in_b)
    rs2_out, rs2_in = (rs2_out_a, rs2_out_b), (rs2_in_a, rs2_in_b)
    ag = (ag_a, ag_b)
    first, second = (x, y), (y, x)

    def dp_at(h, f, s):
        return f * side + s if h == 0 else s * side + f

    def ahead(v, k, n):
        return lax.rem(v + k, n)

    def behind(v, k, n):
        return lax.rem(v + n - k, n)

    def remote(src, dst, send, recv, **to):
        return pltpu.make_async_remote_copy(
            src_ref=src, dst_ref=dst, send_sem=send, recv_sem=recv, device_id=to, device_id_type=MESH)

    def z_offset(j):
        return n_mp // 2 + ((j + 1) // 2) * (1 - 2 * lax.rem(j, 2))

    loads = [
        pltpu.make_async_copy(src, dst, in_sem.at[i])
        for i, (src, dst) in enumerate((
            (grad_hbm, grad_ref), (owners_hbm, owners_ref), (mom_hbm, mom_ref), (master_hbm, master_ref)))
    ]
    for load in loads:
        load.start()

    barrier = pltpu.get_barrier_semaphore()

    @pl.loop(1, n_dp)
    def _(k):
        pl.semaphore_signal(barrier, 1, device_id={"dp": ahead(dp, k, n_dp)}, device_id_type=MESH)

    @pl.loop(1, n_mp)
    def _(k):
        pl.semaphore_signal(barrier, 1, device_id={"mp": ahead(mp, k, n_mp)}, device_id_type=MESH)

    loads[0].wait()

    @pl.loop(0, blocks)
    def _(b):
        at = pl.ds(pl.multiple_of(b * shard, 16), shard)
        wide[at, :] = grad_ref[at, :].astype(F32)

    def pick(q, h, f, dst):
        @pl.loop(0, side)
        def _(s):
            base = h * half * shard + dp_at(h, f, s) * rows + starts[q]
            for r in range(counts[q]):
                dst[s, r] = wide[pl.ds(base + r, half, stride=shard), :].astype(BF16)

    loads[1].wait()
    lane = lax.broadcasted_iota(jnp.int32, (8, 128), 1)
    owner_row = jnp.full((8, 128), -1, jnp.int32)
    for b in range(blocks):
        owner_row = jnp.where(lane == b, owners_ref[b], owner_row)
    position = jnp.zeros((8, 128), jnp.int32)
    for b in range(blocks):
        position = position + jnp.where((owner_row == owners_ref[b]) & (lane > b), 1, 0)
    slot_row = jnp.where(owner_row >= 0, owner_row * cap + position, -1)[0:1, 0:blocks]
    place = jnp.broadcast_to(slot_row, (slots, blocks)) == lax.broadcasted_iota(jnp.int32, (slots, blocks), 0)
    onehot = jnp.where(place, 1.0, 0.0).astype(F32)
    onehot_t = onehot.T.astype(BF16)
    onehot = onehot.astype(BF16)
    count = jnp.int32(0)
    for b in range(blocks):
        count = count + jnp.where(owners_ref[b] == mp, 1, 0)

    pl.semaphore_wait(barrier, n_dp + n_mp - 2)

    def rs1(q, h, k, f):
        return remote(rs1_out[q].at[h, f], rs1_in[q].at[h, first[h]], rs1_s.at[q, h, k], rs1_r.at[q, h, k],
                      dp=dp_at(h, f, second[h]))

    def rs2(q, h, k, s):
        return remote(rs2_out[q].at[h, s], rs2_in[q].at[h, second[h]], rs2_s.at[q, h, k], rs2_r.at[q, h, k],
                      dp=dp_at(h, first[h], s))

    for q in (few, many):
        for k in range(1, side):
            for h in range(2):
                f = ahead(first[h], k, side)
                pick(q, h, f, rs1_out[q].at[h, f])
                rs1(q, h, k, f).start()
        for h in range(2):
            pick(q, h, first[h], rs1_in[q].at[h, first[h]])

    z32[...] = jnp.zeros_like(z32)

    for q in (few, many):
        for h in range(2):
            for k in range(1, side):
                f = behind(first[h], k, side)
                remote(rs1_out[q].at[h, f], rs1_in[q].at[h, f], rs1_s.at[q, h, k], rs1_r.at[q, h, k],
                       dp=dp_at(h, f, second[h])).wait_recv()
            for k in range(1, side + 1):
                s = ahead(second[h], k, side)
                for r in range(counts[q]):
                    total = rs1_in[q][h, 0, s, r].astype(F32)
                    for f in range(1, side):
                        total = total + rs1_in[q][h, f, s, r].astype(F32)
                    if k < side:
                        rs2_out[q][h, s, r] = total.astype(BF16)
                    else:
                        rs2_in[q][h, s, r] = total.astype(BF16)
                if k < side:
                    rs2(q, h, k, s).start()

    def z_copy(j, q, src, dst, s, r):
        to = ahead(mp, z_offset(j), n_mp)
        return remote(src.at[q, to], dst.at[q, mp], s.at[q, j], r.at[q, j], mp=to)

    def z_send(q, src, dst, s, r):
        @pl.loop(0, n_mp - 1)
        def _(j):
            z_copy(j, q, src, dst, s, r).start()

        dst[q, mp] = src[q, mp]

    def z_wait(q, src, dst, s, r):
        @pl.loop(0, n_mp - 1)
        def _(j):
            source = behind(mp, z_offset(j), n_mp)
            remote(src.at[q, source], dst.at[q, source], s.at[q, j], r.at[q, j], mp=source).wait_recv()

    for q in (few, many):
        for h in range(2):
            for k in range(1, side):
                s = behind(second[h], k, side)
                remote(rs2_out[q].at[h, s], rs2_in[q].at[h, s], rs2_s.at[q, h, k], rs2_r.at[q, h, k],
                       dp=dp_at(h, first[h], s)).wait_recv()
        for r in range(counts[q]):
            both = []
            for h in range(2):
                total = rs2_in[q][h, 0, r].astype(F32)
                for s in range(1, side):
                    total = total + rs2_in[q][h, s, r].astype(F32)
                both.append(total)
            total = jnp.concatenate(both, axis=0).astype(BF16)
            z32[pl.ds(r, slots, stride=8), :] = jnp.dot(onehot, total, preferred_element_type=F32)
        z_out[q] = z32[...].astype(BF16).reshape(n_mp, cap * 8, 128)
        z_send(q, z_out, z_in, z_s, z_r)

    loads[2].wait()
    loads[3].wait()
    for q in (few, many):
        z_wait(q, z_out, z_in, z_s, z_r)
        z32[...] = z_in[q].reshape(z32.shape).astype(F32)
        for c in range(cap):
            for j in range(counts[q]):
                r = starts[q] + j
                arrived = z32[pl.ds(c * 8 + j, n_mp, stride=cap * 8), :]
                before = mom_ref[c, r]
                after = (decay_rate * before.astype(F32) + arrived).astype(BF16)
                newmom_ref[c, r] = jnp.where(count > c, after, before)
                upd[c, pl.ds(r * n_mp, n_mp), :] = arrived + decay_rate * after.astype(F32)

    piece = 128 // n_dp
    for c in range(cap):
        u = upd[c]
        gram = lax.dot_general(u, u, (((0,), (0,)), ((), ())), precision=lax.Precision.HIGHEST,
                               preferred_element_type=F32)
        for d in range(n_dp):
            gram_out[d, c] = gram[d * piece:(d + 1) * piece, :]

    @pl.loop(1, n_dp)
    def _(k):
        to = ahead(dp, k, n_dp)
        remote(gram_out.at[to], gram_in.at[dp], g_s.at[k], g_r.at[k], dp=to).start()

    gram_in[dp] = gram_out[dp]

    @pl.loop(1, n_dp)
    def _(k):
        source = behind(dp, k, n_dp)
        remote(gram_out.at[source], gram_in.at[source], g_s.at[k], g_r.at[k], dp=source).wait_recv()

    part = gram_in[0]
    for s in range(1, n_dp):
        part = part + gram_in[s]
    gram_all[dp] = part

    @pl.loop(1, n_dp)
    def _(k):
        to = ahead(dp, k, n_dp)
        remote(gram_all.at[dp], gram_all.at[dp], h_s.at[k], h_r.at[k], dp=to).start()

    @pl.loop(1, n_dp)
    def _(k):
        source = behind(dp, k, n_dp)
        remote(gram_all.at[source], gram_all.at[source], h_s.at[k], h_r.at[k], dp=source).wait_recv()

    eye = lax.broadcasted_iota(jnp.int32, (128, 128), 0) == lax.broadcasted_iota(jnp.int32, (128, 128), 1)
    a0, a1, a2 = NEWTON
    grams, norms = [], []
    for c in range(cap):
        raw = gram_all[:, c].reshape(128, 128)
        norm = jnp.sqrt(jnp.sum(jnp.where(eye, raw, 0.0), axis=(0, 1), keepdims=True)) + 1e-07
        grams.append(raw / (norm * norm))
        norms.append(norm)
    polys = [None] * cap
    for i in range(ITERS):
        mixes = [a1 * g + a2 * dot(g, g) for g in grams]
        if i == 0:
            polys = [jnp.where(eye, a0, 0.0) + m for m in mixes]
        else:
            polys = [a0 * p + dot(p, m) for p, m in zip(polys, mixes)]
        if i < ITERS - 1:
            halves = [a0 * g + dot(m, g) for g, m in zip(grams, mixes)]
            grams = [a0 * h + dot(h, m) for h, m in zip(halves, mixes)]
    polys = [p * (-learn_rate * update_gain * math.sqrt(D) / n) for p, n in zip(polys, norms)]

    peaks = [jnp.zeros((n_mp, 128), F32)] * cap
    for q in (many, few):
        for c in range(cap):
            at, size = starts[q] * n_mp, counts[q] * n_mp
            step = dot(upd[c, at:at + size, :], polys[c])
            for j in range(counts[q]):
                r = starts[q] + j
                before = master_ref[c, r]
                after = before * (1.0 - learn_rate * weight_decay) + step[j * n_mp:(j + 1) * n_mp, :]
                newmaster_ref[c, r] = jnp.where(count > c, after, before)
                peaks[c] = jnp.maximum(peaks[c], jnp.abs(after))
                z32[pl.ds(c * 8 + j, n_mp, stride=cap * 8), :] = after
            if q == few:
                peak = jnp.broadcast_to(jnp.max(peaks[c], axis=(0, 1), keepdims=True), (n_mp, 128))
                high = peak.astype(BF16).astype(F32)
                low = peak - high
                left = lax.broadcasted_iota(jnp.int32, (n_mp, 128), 1) < 64
                z32[pl.ds(c * 8 + counts[q], n_mp, stride=cap * 8), :] = jnp.where(left, high, low)
        y_out[q] = z32[...].astype(BF16).reshape(n_mp, cap * 8, 128)
        z_send(q, y_out, y_in, y_s, y_r)

    def ag1(q, h, k, f, p):
        at = ag[q].at[h, second[h], f]
        return remote(at, at, ag1_s.at[q, h, k], ag1_r.at[q, h, k], dp=dp_at(h, p, second[h]))

    def ag2(q, h, k, s, p):
        at = ag[q].at[h, s]
        return remote(at, at, ag2_s.at[q, h, k], ag2_r.at[q, h, k], dp=dp_at(h, first[h], p))

    sent = (counts[0] + 1, counts[1])
    for q in (many, few):
        z_wait(q, y_out, y_in, y_s, y_r)
        z32[...] = y_in[q].reshape(z32.shape).astype(F32)
        for r in range(sent[q]):
            v = z32[pl.ds(r, slots, stride=8), :].astype(BF16)
            v = jnp.dot(onehot_t, v, preferred_element_type=F32)
            for h in range(2):
                ag[q][h, second[h], first[h], r] = v[h * half:(h + 1) * half, :].astype(BF16)
        for k in range(1, side):
            for h in range(2):
                ag1(q, h, k, first[h], ahead(first[h], k, side)).start()
        for h in range(2):
            for k in range(1, side):
                f = behind(first[h], k, side)
                ag1(q, h, k, f, f).wait_recv()
            for k in range(1, side):
                ag2(q, h, k, second[h], ahead(second[h], k, side)).start()

    def spread(q, h, s):
        @pl.loop(0, side)
        def _(f):
            base = h * half * shard + dp_at(h, f, s) * rows + starts[q]
            for r in range(counts[q]):
                wide[pl.ds(base + r, half, stride=shard), :] = ag[q][h, s, f, r].astype(F32)

    for q in (many, few):
        for h in range(2):
            spread(q, h, second[h])
    for q in (many, few):
        for k in range(1, side):
            for h in range(2):
                s = behind(second[h], k, side)
                ag2(q, h, k, s, s).wait_recv()
                spread(q, h, s)

    both = []
    for h in range(2):
        peak = jnp.zeros((half, 128), F32)
        for s in range(side):
            for f in range(side):
                v = ag[few][h, s, f, counts[few]].astype(F32)
                peak = jnp.maximum(peak, v + pltpu.roll(v, 64, 1))
        both.append(peak)
    peak = jnp.concatenate(both, axis=0) + 1e-06
    z32[0:blocks, :] = 1.0 / peak
    scale_ref[...] = peak

    @pl.loop(0, blocks)
    def _(b):
        at = pl.ds(pl.multiple_of(b * shard, 16), shard)
        out_ref[at, :] = (wide[at, :] * z32[pl.ds(b, 1), :]).astype(BF16)

    for q in range(2):
        for h in range(2):
            for k in range(1, side):
                f, s = ahead(first[h], k, side), ahead(second[h], k, side)
                rs1(q, h, k, f).wait_send()
                rs2(q, h, k, s).wait_send()
                ag1(q, h, k, first[h], f).wait_send()
                ag2(q, h, k, second[h], s).wait_send()

    @pl.loop(1, n_dp)
    def _(k):
        to = ahead(dp, k, n_dp)
        remote(gram_out.at[to], gram_in.at[dp], g_s.at[k], g_r.at[k], dp=to).wait_send()
        remote(gram_all.at[dp], gram_all.at[dp], h_s.at[k], h_r.at[k], dp=to).wait_send()

    @pl.loop(0, n_mp - 1)
    def _(j):
        for q in range(2):
            z_copy(j, q, z_out, z_in, z_s, z_r).wait_send()
            z_copy(j, q, y_out, y_in, y_s, y_r).wait_send()


def body(gradients, owners, momentum, master):
    n_dp, n_mp = lax.axis_size("dp"), lax.axis_size("mp")
    _, blocks, shard, head = gradients.shape
    cap, _, rows, _ = momentum.shape
    slots = n_mp * cap
    moved = (cap, rows, n_mp, head)
    few, many, half = rows - 8, 8, blocks // 2
    sem = pltpu.SemaphoreType.DMA
    vmem = pl.BlockSpec(memory_space=pltpu.VMEM)
    out, scale, newmom, newmaster = pl.pallas_call(
        functools.partial(kernel, n_dp, n_mp, cap, blocks, rows),
        out_shape=(
            jax.ShapeDtypeStruct((blocks * shard, head), BF16),
            jax.ShapeDtypeStruct((blocks, head), F32),
            jax.ShapeDtypeStruct(moved, BF16),
            jax.ShapeDtypeStruct(moved, F32),
        ),
        in_specs=[pl.BlockSpec(memory_space=pl.ANY)] * 4,
        out_specs=(vmem,) * 4,
        scratch_shapes=[
            pltpu.SMEM((blocks,), jnp.int32),
            pltpu.VMEM((blocks * shard, head), BF16),
            pltpu.VMEM(moved, BF16),
            pltpu.VMEM(moved, F32),
            pltpu.VMEM((blocks * shard, head), F32),
            *[pltpu.VMEM((2, SIDE, SIDE, n, half, head), BF16) for n in (few, many)],
            *[pltpu.VMEM((2, SIDE, SIDE, n, half, head), BF16) for n in (few, many)],
            *[pltpu.VMEM((2, SIDE, n, half, head), BF16) for n in (few, many)],
            *[pltpu.VMEM((2, SIDE, n, half, head), BF16) for n in (few, many)],
            pltpu.VMEM((slots * 8, head), F32),
            pltpu.VMEM((2, n_mp, cap * 8, head), BF16),
            pltpu.VMEM((2, n_mp, cap * 8, head), BF16),
            pltpu.VMEM((cap, rows * n_mp, head), F32),
            *[pltpu.VMEM((n_dp, cap, head // n_dp, head), F32)] * 3,
            pltpu.VMEM((2, n_mp, cap * 8, head), BF16),
            pltpu.VMEM((2, n_mp, cap * 8, head), BF16),
            *[pltpu.VMEM((2, SIDE, SIDE, n, half, head), BF16) for n in (few + 1, many)],
            sem((4,)),
            *[sem((2, 2, SIDE))] * 4,
            *[sem((2, n_mp))] * 2,
            *[sem((n_dp,))] * 4,
            *[sem((2, n_mp))] * 2,
            *[sem((2, 2, SIDE))] * 4,
        ],
        compiler_params=pltpu.CompilerParams(
            collective_id=0, has_side_effects=True, vmem_limit_bytes=48 * 2**20),
        name="muon_step",
    )(
        owners,
        gradients.reshape(blocks * shard, head),
        momentum.transpose(0, 2, 1, 3),
        master.transpose(0, 2, 1, 3),
    )
    return (
        out.reshape(blocks, shard, head),
        scale[:, 0],
        newmom.transpose(0, 2, 1, 3),
        newmaster.transpose(0, 2, 1, 3),
    )


def solution(mesh):
    in_specs = (
        P("dp", None, "mp", None),
        P(),
        P("mp", None, "dp", None),
        P("mp", None, "dp", None),
    )
    out_specs = (P(None, "mp", None), P(), P("mp", None, "dp", None), P("mp", None, "dp", None))
    return jax.shard_map(body, mesh=mesh, in_specs=in_specs, out_specs=out_specs, check_vma=False)
```

time: 145 us -> 105 us (0.72)
  the two profiles are of different devices: /device:TPU:28 before, /device:TPU:1 now
where the time goes in v2:
time: 105 us
  Pallas kernels  97 us (92%)
  local copies, waits for them, and re-layouts  7.41 us (7%)
    pallas_call x1, Pallas kernels, body(): pl.pallas_call(functools.partial(kernel, n_dp, n_mp, cap, blocks, rows),...  97 us
    unnamed x11, local copies, waits for them, and re-layouts  6.79 us

profile of v2, /device:TPU:1, one launch (start us, length us, event | category | flops | bytes accessed | tf_op | source)
XLA Modules:
  0.0 105.1 jit_solution(2092499540689882099)
XLA Ops:
  0.6 0.0 copy-start
  0.6 1.5 %copy-done = bf16[1,32,224,128]{3,2,1,0:T(8,128)(2,1)S(1)} copy-done((bf16[1,32,224,128]{3,2,1,0:T(8,128)(2,1)S(1)}, bf16[1,32,224,128]{3,2,1,0:T(8,128)(2,1)}, u32[]{:S(2)}) %copy-start) | copy-done | bytes 1835032
  2.1 0.0 copy-start.1
  2.1 1.0 copy-done.1
  3.2 0.0 copy-start.2
  3.2 0.9 copy-done.2
  4.1 0.0 copy-start.3
  4.1 0.7 copy-done.3
  4.7 97.0 %muon_step.1 = (bf16[7168,128]{1,0:T(8,128)(2,1)S(1)}, f32[32,128]{1,0:T(8,128)S(1)}, bf16[2,14,32,128]{3,2,1,0:T(8,128)(2,1)S(1)}, f32[2,14,32,128]{3,2,1,0:T(8,128)S(1)}) custom-call(s32[32]{0:T(128)S(1)} %copy-done.3, bf16[7168,128]{1,0:T(8,128)(2,1)S(1)} %bitcast.7, bf16[2,14,32,128]{3,2,1,0:T(8,128)(2,1)S(1)} %bitcast.11, f32[2,14,32,128]{3,2,1,0:T(8,128)S(1)} %bitcast.9), custom_call_target="tpu_custom_call" | custom-call | tf_op jit(solution)/shard_map/muon_step/pallas_call | solution.py:371
  101.8 0.6 slice_reduce_fusion
  102.4 1.2 %copy.11 = bf16[32,224,128]{2,1,0:T(8,128)(2,1)} copy(bf16[32,224,128]{2,1,0:T(8,128)(2,1)S(1)} %bitcast.6) | data formatting | bytes 3670016
  103.6 0.7 copy.12
  104.3 0.8 copy.13
Async XLA Ops:
  0.6 1.5 %copy-start = (bf16[1,32,224,128]{3,2,1,0:T(8,128)(2,1)S(1)}, bf16[1,32,224,128]{3,2,1,0:T(8,128)(2,1)}, u32[]{:S(2)}) copy-start(bf16[1,32,224,128]{3,2,1,0:T(8,128)(2,1)} %param.4) | copy-start | bytes 5505028
  2.1 1.0 copy-start.1
  3.2 0.9 copy-start.2
  4.1 0.7 copy-start.3

commit v3 on v2

v3 whole, which is shorter than its diff:
```python
import functools
import math

import jax
import jax.numpy as jnp
from jax import lax
from jax.experimental import pallas as pl
from jax.experimental.pallas import tpu as pltpu
from jax.sharding import PartitionSpec as P

D = 7168
ITERS = 5
NEWTON = (3.4445, -4.775, 2.0315)
decay_rate = 0.95
learn_rate = 0.05
weight_decay = 0.1
update_gain = 0.2

MESH = pl.DeviceIdType.MESH
F32 = jnp.float32
BF16 = jnp.bfloat16
VMEM = 63 * 2**20
SIDE = 4


def dot(a, b):
    return jnp.dot(a, b, precision=lax.Precision.HIGHEST, preferred_element_type=F32)


def kernel(n_dp, n_mp, cap, blocks, rows, owners_hbm, grad_hbm, mom_hbm, master_hbm,
           out_hbm, scale_ref, newmom_hbm, newmaster_hbm,
           owners_ref, grad_ref, mom_ref, master_ref, wide, newmom_ref, newmaster_ref,
           rs1_out_a, rs1_out_b, rs1_in_a, rs1_in_b, rs2_out_a, rs2_out_b, rs2_in_a, rs2_in_b,
           z32, z_out, z_in, upd, gram_out, gram_in, gram_all, y_out, y_in, ag_a, ag_b,
           in_sem, out_sem, rs1_s, rs1_r, rs2_s, rs2_r, z_s, z_r, g_s, g_r, h_s, h_r, y_s, y_r,
           ag1_s, ag1_r, ag2_s, ag2_r):
    dp, mp = lax.axis_index("dp"), lax.axis_index("mp")
    side = SIDE
    x, y = dp // side, lax.rem(dp, side)
    slots = n_mp * cap
    shard = n_dp * rows
    half = blocks // 2
    few, many = 0, 1
    starts, counts = (8, 0), (rows - 8, 8)
    rs1_out, rs1_in = (rs1_out_a, rs1_out_b), (rs1_in_a, rs1_in_b)
    rs2_out, rs2_in = (rs2_out_a, rs2_out_b), (rs2_in_a, rs2_in_b)
    ag = (ag_a, ag_b)
    first, second = (x, y), (y, x)

    def dp_at(h, f, s):
        return f * side + s if h == 0 else s * side + f

    def ahead(v, k, n):
        return lax.rem(v + k, n)

    def behind(v, k, n):
        return lax.rem(v + n - k, n)

    def remote(src, dst, send, recv, **to):
        return pltpu.make_async_remote_copy(
            src_ref=src, dst_ref=dst, send_sem=send, recv_sem=recv, device_id=to, device_id_type=MESH)

    def all_sent(ref, sem):
        remote(ref, ref, sem, sem, dp=ahead(dp, 1, n_dp)).wait_send()

    def all_here(ref, sem):
        remote(ref, ref, sem, sem, dp=ahead(dp, 1, n_dp)).wait_recv()

    def z_offset(j):
        return n_mp // 2 + ((j + 1) // 2) * (1 - 2 * lax.rem(j, 2))

    loads = [
        pltpu.make_async_copy(src, dst, in_sem.at[i])
        for i, (src, dst) in enumerate((
            (grad_hbm.at[0:half * shard], grad_ref.at[0:half * shard]),
            (grad_hbm.at[half * shard:], grad_ref.at[half * shard:]),
            (owners_hbm, owners_ref), (mom_hbm, mom_ref), (master_hbm, master_ref)))
    ]
    for load in loads:
        load.start()

    barrier = pltpu.get_barrier_semaphore()

    @pl.loop(1, n_dp)
    def _(k):
        pl.semaphore_signal(barrier, 1, device_id={"dp": ahead(dp, k, n_dp)}, device_id_type=MESH)

    for h in range(2):
        loads[h].wait()

        @pl.loop(0, half)
        def _(i):
            if h == 0:
                pl.semaphore_signal(barrier, 1, device_id={"mp": ahead(mp, i + 1, n_mp)}, device_id_type=MESH)
            else:

                @pl.when(i > 0)
                def _():
                    pl.semaphore_signal(barrier, 1, device_id={"mp": behind(mp, i, n_mp)}, device_id_type=MESH)

            at = pl.ds(pl.multiple_of((h * half + i) * shard, 16), shard)
            wide[at, :] = grad_ref[at, :].astype(F32)

    def pick(q, h, f, dst):
        @pl.loop(0, side)
        def _(s):
            base = h * half * shard + dp_at(h, f, s) * rows + starts[q]
            for r in range(counts[q]):
                dst[s, r] = wide[pl.ds(base + r, half, stride=shard), :].astype(BF16)

    pl.semaphore_wait(barrier, n_dp + n_mp - 2)

    def rs1(q, h, f):
        return remote(rs1_out[q].at[h, f], rs1_in[q].at[h, first[h]], rs1_s.at[q, h], rs1_r.at[q, h],
                      dp=dp_at(h, f, second[h]))

    def rs2(q, h, s):
        return remote(rs2_out[q].at[h, s], rs2_in[q].at[h, second[h]], rs2_s.at[q, h], rs2_r.at[q, h],
                      dp=dp_at(h, first[h], s))

    for q in (few, many):
        for k in range(1, side):
            for h in range(2):
                f = ahead(first[h], k, side)
                pick(q, h, f, rs1_out[q].at[h, f])
                rs1(q, h, f).start()
        for h in range(2):
            pick(q, h, first[h], rs1_in[q].at[h, first[h]])

    loads[2].wait()
    lane = lax.broadcasted_iota(jnp.int32, (8, 128), 1)
    owner_row = jnp.full((8, 128), -1, jnp.int32)
    for b in range(blocks):
        owner_row = jnp.where(lane == b, owners_ref[b], owner_row)
    position = jnp.zeros((8, 128), jnp.int32)
    for b in range(blocks):
        position = position + jnp.where((owner_row == owners_ref[b]) & (lane > b), 1, 0)
    slot_row = jnp.where(owner_row >= 0, owner_row * cap + position, -1)[0:1, 0:blocks]
    place = jnp.broadcast_to(slot_row, (slots, blocks)) == lax.broadcasted_iota(jnp.int32, (slots, blocks), 0)
    onehot = jnp.where(place, 1.0, 0.0).astype(F32)
    onehot_t = onehot.T.astype(BF16)
    onehot = onehot.astype(BF16)
    count = jnp.int32(0)
    for b in range(blocks):
        count = count + jnp.where(owners_ref[b] == mp, 1, 0)

    z32[...] = jnp.zeros_like(z32)

    for q in (few, many):
        for h in range(2):
            all_here(rs1_in[q].at[h, 0:side - 1], rs1_r.at[q, h])
            for k in range(1, side + 1):
                s = ahead(second[h], k, side)
                for r in range(counts[q]):
                    total = rs1_in[q][h, 0, s, r].astype(F32)
                    for f in range(1, side):
                        total = total + rs1_in[q][h, f, s, r].astype(F32)
                    if k < side:
                        rs2_out[q][h, s, r] = total.astype(BF16)
                    else:
                        rs2_in[q][h, s, r] = total.astype(BF16)
                if k < side:
                    rs2(q, h, s).start()

    def z_copy(j, q, src, dst, s, r):
        to = ahead(mp, z_offset(j), n_mp)
        return remote(src.at[q, to], dst.at[q, mp], s.at[q], r.at[q], mp=to)

    def z_send(q, src, dst, s, r):
        @pl.loop(0, n_mp - 1)
        def _(j):
            z_copy(j, q, src, dst, s, r).start()

        dst[q, mp] = src[q, mp]

    for q in (few, many):
        for h in range(2):
            all_here(rs2_in[q].at[h, 0:side - 1], rs2_r.at[q, h])
        for r in range(counts[q]):
            both = []
            for h in range(2):
                total = rs2_in[q][h, 0, r].astype(F32)
                for s in range(1, side):
                    total = total + rs2_in[q][h, s, r].astype(F32)
                both.append(total)
            total = jnp.concatenate(both, axis=0).astype(BF16)
            z32[pl.ds(r, slots, stride=8), :] = jnp.dot(onehot, total, preferred_element_type=F32)
        z_out[q] = z32[...].astype(BF16).reshape(n_mp, cap * 8, 128)
        z_send(q, z_out, z_in, z_s, z_r)

    loads[3].wait()
    loads[4].wait()
    for q in (few, many):
        all_here(z_in.at[q, 0:n_mp - 1], z_r.at[q])
        z32[...] = z_in[q].reshape(z32.shape).astype(F32)
        for c in range(cap):
            for j in range(counts[q]):
                r = starts[q] + j
                arrived = z32[pl.ds(c * 8 + j, n_mp, stride=cap * 8), :]
                before = mom_ref[c, r]
                after = (decay_rate * before.astype(F32) + arrived).astype(BF16)
                newmom_ref[c, r] = jnp.where(count > c, after, before)
                upd[c, pl.ds(r * n_mp, n_mp), :] = arrived + decay_rate * after.astype(F32)

    stores = [pltpu.make_async_copy(newmom_ref, newmom_hbm, out_sem.at[0])]
    stores[0].start()

    piece = 128 // n_dp
    for c in range(cap):
        u = upd[c]
        gram = lax.dot_general(u, u, (((0,), (0,)), ((), ())), precision=lax.Precision.HIGHEST,
                               preferred_element_type=F32)
        for d in range(n_dp):
            gram_out[d, c] = gram[d * piece:(d + 1) * piece, :]

    @pl.loop(1, n_dp)
    def _(k):
        to = ahead(dp, k, n_dp)
        remote(gram_out.at[to], gram_in.at[dp], g_s, g_r, dp=to).start()

    gram_in[dp] = gram_out[dp]

    all_here(gram_in.at[0:n_dp - 1], g_r)

    part = gram_in[0]
    for s in range(1, n_dp):
        part = part + gram_in[s]
    gram_all[dp] = part

    @pl.loop(1, n_dp)
    def _(k):
        to = ahead(dp, k, n_dp)
        remote(gram_all.at[dp], gram_all.at[dp], h_s, h_r, dp=to).start()

    all_here(gram_all.at[0:n_dp - 1], h_r)

    eye = lax.broadcasted_iota(jnp.int32, (128, 128), 0) == lax.broadcasted_iota(jnp.int32, (128, 128), 1)
    a0, a1, a2 = NEWTON
    grams, norms = [], []
    for c in range(cap):
        raw = gram_all[:, c].reshape(128, 128)
        norm = jnp.sqrt(jnp.sum(jnp.where(eye, raw, 0.0), axis=(0, 1), keepdims=True)) + 1e-07
        grams.append(raw / (norm * norm))
        norms.append(norm)
    polys = [None] * cap
    for i in range(ITERS):
        mixes = [a1 * g + a2 * dot(g, g) for g in grams]
        if i == 0:
            polys = [jnp.where(eye, a0, 0.0) + m for m in mixes]
        else:
            polys = [a0 * p + dot(p, m) for p, m in zip(polys, mixes)]
        if i < ITERS - 1:
            halves = [a0 * g + dot(m, g) for g, m in zip(grams, mixes)]
            grams = [a0 * h + dot(h, m) for h, m in zip(halves, mixes)]
    polys = [p * (-learn_rate * update_gain * math.sqrt(D) / n) for p, n in zip(polys, norms)]

    peaks = [jnp.zeros((n_mp, 128), F32)] * cap
    for q in (many, few):
        for c in range(cap):
            at, size = starts[q] * n_mp, counts[q] * n_mp
            step = dot(upd[c, at:at + size, :], polys[c])
            for j in range(counts[q]):
                r = starts[q] + j
                before = master_ref[c, r]
                after = before * (1.0 - learn_rate * weight_decay) + step[j * n_mp:(j + 1) * n_mp, :]
                newmaster_ref[c, r] = jnp.where(count > c, after, before)
                peaks[c] = jnp.maximum(peaks[c], jnp.abs(after))
                z32[pl.ds(c * 8 + j, n_mp, stride=cap * 8), :] = after
            if q == few:
                peak = jnp.broadcast_to(jnp.max(peaks[c], axis=(0, 1), keepdims=True), (n_mp, 128))
                high = peak.astype(BF16).astype(F32)
                low = peak - high
                left = lax.broadcasted_iota(jnp.int32, (n_mp, 128), 1) < 64
                z32[pl.ds(c * 8 + counts[q], n_mp, stride=cap * 8), :] = jnp.where(left, high, low)
        y_out[q] = z32[...].astype(BF16).reshape(n_mp, cap * 8, 128)
        z_send(q, y_out, y_in, y_s, y_r)

    stores.append(pltpu.make_async_copy(newmaster_ref, newmaster_hbm, out_sem.at[1]))
    stores[1].start()

    def ag1(q, h, k, p):
        return remote(ag[q].at[h, second[h], 0], ag[q].at[h, second[h], k], ag1_s.at[q, h], ag1_r.at[q, h],
                      dp=dp_at(h, p, second[h]))

    def ag2(q, h, s, p, part):
        at = ag[q].at[h, s, 0] if part == 0 else ag[q].at[h, s, pl.ds(1, side - 1)]
        return remote(at, at, ag2_s.at[q, h, part], ag2_r.at[q, h, part], dp=dp_at(h, first[h], p))

    sent = (counts[0] + 1, counts[1])
    for q in (many, few):
        all_here(y_in.at[q, 0:n_mp - 1], y_r.at[q])
        z32[...] = y_in[q].reshape(z32.shape).astype(F32)
        for r in range(sent[q]):
            v = z32[pl.ds(r, slots, stride=8), :].astype(BF16)
            v = jnp.dot(onehot_t, v, preferred_element_type=F32)
            for h in range(2):
                ag[q][h, second[h], 0, r] = v[h * half:(h + 1) * half, :].astype(BF16)
        for k in range(1, side):
            for h in range(2):
                ag1(q, h, k, ahead(first[h], k, side)).start()
        for k in range(1, side):
            for h in range(2):
                ag2(q, h, second[h], ahead(second[h], k, side), 0).start()
        for h in range(2):
            all_here(ag[q].at[h, second[h], 1:side], ag1_r.at[q, h])
            for k in range(1, side):
                ag2(q, h, second[h], ahead(second[h], k, side), 1).start()

    def spread(q, h, s, k):
        f = behind(first[h], k, side)
        base = h * half * shard + dp_at(h, f, s) * rows + starts[q]
        for r in range(counts[q]):
            wide[pl.ds(base + r, half, stride=shard), :] = ag[q][h, s, k, r].astype(F32)

    for q in (many, few):
        for h in range(2):
            for k in range(side):
                spread(q, h, second[h], k)
    for q in (many, few):
        for part in range(2):
            for h in range(2):
                all_here(ag[q].at[h, 0:side - 1, 0] if part == 0 else ag[q].at[h, 0:side - 1, 1:side], ag2_r.at[q, h, part])
                for k in range(1, side):
                    s = behind(second[h], k, side)
                    if part == 0:
                        spread(q, h, s, 0)
                    else:
                        pl.loop(1, side)(functools.partial(spread, q, h, s))

    both = []
    for h in range(2):
        peak = jnp.zeros((half, 128), F32)
        for s in range(side):
            for f in range(side):
                v = ag[few][h, s, f, counts[few]].astype(F32)
                peak = jnp.maximum(peak, v + pltpu.roll(v, 64, 1))
        both.append(peak)
    peak = jnp.concatenate(both, axis=0) + 1e-06
    scale_ref[...] = peak.T[0:1, :]
    z32[0:blocks, :] = 1.0 / peak
    parts = 4
    step = blocks // parts
    for i in range(parts):

        @pl.loop(i * step, i * step + step)
        def _(b):
            at = pl.ds(pl.multiple_of(b * shard, 16), shard)
            grad_ref[at, :] = (wide[at, :] * z32[pl.ds(b, 1), :]).astype(BF16)

        part = pl.ds(i * step * shard, step * shard)
        stores.append(pltpu.make_async_copy(grad_ref.at[part], out_hbm.at[part], out_sem.at[2 + i]))
        stores[-1].start()
    for store in stores:
        store.wait()

    for q in range(2):
        all_sent(z_out.at[q, 0:n_mp - 1], z_s.at[q])
        all_sent(y_out.at[q, 0:n_mp - 1], y_s.at[q])
        for h in range(2):
            all_sent(rs1_out[q].at[h, 0:side - 1], rs1_s.at[q, h])
            all_sent(rs2_out[q].at[h, 0:side - 1], rs2_s.at[q, h])
            all_sent(ag[q].at[h, 0, 1:side], ag1_s.at[q, h])
            all_sent(ag[q].at[h, 0:side - 1, 0], ag2_s.at[q, h, 0])
            all_sent(ag[q].at[h, 0:side - 1, 1:side], ag2_s.at[q, h, 1])
    all_sent(gram_out.at[0:n_dp - 1], g_s)
    all_sent(gram_all.at[0:n_dp - 1], h_s)


def finish(out_in, scale_in, newmom_in, newmaster_in, out_hbm, scale_hbm, newmom_hbm, newmaster_hbm,
           out_ref, scale_ref, newmom_ref, newmaster_ref, in_sem, out_sem):
    parts = 4
    step = out_ref.shape[0] // parts
    ways = [(scale_in, scale_ref, scale_hbm)]
    for i in range(parts):
        at = pl.ds(i * step, step)
        ways.append((out_in.at[at], out_ref.at[at], out_hbm.at[at]))
    ways += [(newmaster_in, newmaster_ref, newmaster_hbm), (newmom_in, newmom_ref, newmom_hbm)]
    loads = [pltpu.make_async_copy(a, b, in_sem.at[i]) for i, (a, b, _) in enumerate(ways)]
    stores = [pltpu.make_async_copy(b, c, out_sem.at[i]) for i, (_, b, c) in enumerate(ways)]
    for load in loads:
        load.start()
    for load, store in zip(loads, stores):
        load.wait()
        store.start()
    for store in stores:
        store.wait()


def body(gradients, owners, momentum, master):
    n_dp, n_mp = lax.axis_size("dp"), lax.axis_size("mp")
    _, blocks, shard, head = gradients.shape
    cap, _, rows, _ = momentum.shape
    slots = n_mp * cap
    moved = (cap, rows, n_mp, head)
    few, many, half = rows - 8, 8, blocks // 2
    sem = pltpu.SemaphoreType.DMA
    hbm = pl.BlockSpec(memory_space=pltpu.HBM)
    vmem = pl.BlockSpec(memory_space=pltpu.VMEM)
    results = pl.pallas_call(
        functools.partial(kernel, n_dp, n_mp, cap, blocks, rows),
        out_shape=(
            jax.ShapeDtypeStruct((blocks * shard, head), BF16),
            jax.ShapeDtypeStruct((1, blocks), F32),
            jax.ShapeDtypeStruct(moved, BF16),
            jax.ShapeDtypeStruct(moved, F32),
        ),
        in_specs=[hbm] * 4,
        out_specs=(hbm, vmem, hbm, hbm),
        scratch_shapes=[
            pltpu.SMEM((blocks,), jnp.int32),
            pltpu.VMEM((blocks * shard, head), BF16),
            pltpu.VMEM(moved, BF16),
            pltpu.VMEM(moved, F32),
            pltpu.VMEM((blocks * shard, head), F32),
            pltpu.VMEM(moved, BF16),
            pltpu.VMEM(moved, F32),
            *[pltpu.VMEM((2, SIDE, SIDE, n, half, head), BF16) for n in (few, many)],
            *[pltpu.VMEM((2, SIDE, SIDE, n, half, head), BF16) for n in (few, many)],
            *[pltpu.VMEM((2, SIDE, n, half, head), BF16) for n in (few, many)],
            *[pltpu.VMEM((2, SIDE, n, half, head), BF16) for n in (few, many)],
            pltpu.VMEM((slots * 8, head), F32),
            pltpu.VMEM((2, n_mp, cap * 8, head), BF16),
            pltpu.VMEM((2, n_mp, cap * 8, head), BF16),
            pltpu.VMEM((cap, rows * n_mp, head), F32),
            *[pltpu.VMEM((n_dp, cap, head // n_dp, head), F32)] * 3,
            pltpu.VMEM((2, n_mp, cap * 8, head), BF16),
            pltpu.VMEM((2, n_mp, cap * 8, head), BF16),
            *[pltpu.VMEM((2, SIDE, SIDE, n, half, head), BF16) for n in (few + 1, many)],
            sem((5,)),
            sem((6,)),
            *[sem((2, 2))] * 4,
            *[sem((2,))] * 2,
            *[sem(())] * 4,
            *[sem((2,))] * 2,
            *[sem((2, 2))] * 2,
            *[sem((2, 2, 2))] * 2,
        ],
        compiler_params=pltpu.CompilerParams(
            collective_id=0, has_side_effects=True, vmem_limit_bytes=VMEM),
        name="muon_step",
    )(
        owners,
        gradients.reshape(blocks * shard, head),
        momentum.transpose(0, 2, 1, 3),
        master.transpose(0, 2, 1, 3),
    )
    out, scale, newmom, newmaster = pl.pallas_call(
        finish,
        out_shape=(
            jax.ShapeDtypeStruct((blocks * shard, head), BF16),
            jax.ShapeDtypeStruct((1, blocks), F32),
            jax.ShapeDtypeStruct(moved, BF16),
            jax.ShapeDtypeStruct(moved, F32),
        ),
        in_specs=[hbm] * 4,
        out_specs=[hbm] * 4,
        scratch_shapes=[
            pltpu.VMEM((blocks * shard, head), BF16),
            pltpu.VMEM((1, blocks), F32),
            pltpu.VMEM(moved, BF16),
            pltpu.VMEM(moved, F32),
            sem((7,)),
            sem((7,)),
        ],
        compiler_params=pltpu.CompilerParams(vmem_limit_bytes=VMEM),
        name="write_results",
    )(*results)
    return (
        out.reshape(blocks, shard, head),
        scale.reshape(blocks),
        newmom.transpose(0, 2, 1, 3),
        newmaster.transpose(0, 2, 1, 3),
    )


def solution(mesh):
    in_specs = (
        P("dp", None, "mp", None),
        P(),
        P("mp", None, "dp", None),
        P("mp", None, "dp", None),
    )
    out_specs = (P(None, "mp", None), P(), P("mp", None, "dp", None), P("mp", None, "dp", None))
    return jax.shard_map(body, mesh=mesh, in_specs=in_specs, out_specs=out_specs, check_vma=False)
```

time: 105 us -> 96 us (0.914)
  the two profiles are of different devices: /device:TPU:1 before, /device:TPU:32 now
where the time goes in v3:
time: 96 us; the launch traced here: 95.8 us
  Pallas kernels  95.2 us (99%)
    pallas_call x1, Pallas kernels, body(): pl.pallas_call(functools.partial(kernel, n_dp, n_mp, cap, blocks, rows),...  92.6 us
    pallas_call x1, Pallas kernels, body(): pl.pallas_call(finish, out_shape=(jax.ShapeDtypeStruct((blocks * shard, h...  2.59 us

profile of v3, /device:TPU:32, one launch (start us, length us, event | category | flops | bytes accessed | tf_op | source)
XLA Modules:
  0.0 95.8 jit_solution(1922238569742983650)
XLA Ops:
  0.6 92.6 %muon_step.1 = (bf16[7168,128]{1,0:T(8,128)(2,1)}, f32[1,32]{1,0:T(1,128)}, bf16[2,14,32,128]{3,2,1,0:T(8,128)(2,1)}, f32[2,14,32,128]{3,2,1,0:T(8,128)}) custom-call(s32[32]{0:T(128)} %owners_hbm.1, bf16[7168,128]{1,0:T(8,128)(2,1)} %bitcast.7, bf16[2,14,32,128]{3,2,1,0:T(8,128)(2,1)} %bitcast.9, f32[2,14,32,128]{3,2,1,0:T(8,128)} %bitcast.8), custom_call_target="tpu_custom_call" | custom-call | tf_op jit(solution)/shard_map/muon_step/pallas_call | solution.py:399
  93.2 2.6 %write_results.1 = (bf16[7168,128]{1,0:T(8,128)(2,1)}, f32[1,32]{1,0:T(1,128)}, bf16[2,14,32,128]{3,2,1,0:T(8,128)(2,1)}, f32[2,14,32,128]{3,2,1,0:T(8,128)}) custom-call(bf16[7168,128]{1,0:T(8,128)(2,1)} %get-tuple-element.12.out_in, f32[1,32]{1,0:T(1,128)} %get-tuple-element.13.scale_in, bf16[2,14,32,128]{3,2,1,0:T(8,128)(2,1)} %get-tuple-element.14.newmom_in, ...), custom_call_target="tpu_custom_call" | custom-call | tf_op jit(solution)/shard_map/write_results/pallas_call | solution.py:447

commit v4 on v3

--- a/solution.py
+++ b/solution.py
@@ -20,6 +20,7 @@
 F32 = jnp.float32
 BF16 = jnp.bfloat16
 VMEM = 63 * 2**20
+NEAR = (1, 2, 8, 13, 19, 24, 30, 31)
 SIDE = 4
 
 
@@ -32,7 +33,7 @@
            owners_ref, grad_ref, mom_ref, master_ref, wide, newmom_ref, newmaster_ref,
            rs1_out_a, rs1_out_b, rs1_in_a, rs1_in_b, rs2_out_a, rs2_out_b, rs2_in_a, rs2_in_b,
            z32, z_out, z_in, upd, gram_out, gram_in, gram_all, y_out, y_in, ag_a, ag_b,
-           in_sem, out_sem, rs1_s, rs1_r, rs2_s, rs2_r, z_s, z_r, g_s, g_r, h_s, h_r, y_s, y_r,
+           near_sem, in_sem, out_sem, rs1_s, rs1_r, rs2_s, rs2_r, z_s, z_r, g_s, g_r, h_s, h_r, y_s, y_r,
            ag1_s, ag1_r, ag2_s, ag2_r):
     dp, mp = lax.axis_index("dp"), lax.axis_index("mp")
     side = SIDE
@@ -81,23 +82,18 @@
 
     barrier = pltpu.get_barrier_semaphore()
 
-    @pl.loop(1, n_dp)
-    def _(k):
-        pl.semaphore_signal(barrier, 1, device_id={"dp": ahead(dp, k, n_dp)}, device_id_type=MESH)
+    for k in range(1, side):
+        for h in range(2):
+            f = ahead(first[h], k, side)
+            pl.semaphore_signal(barrier, 1, device_id={"dp": dp_at(h, f, second[h])}, device_id_type=MESH)
+    for k in NEAR:
+        pl.semaphore_signal(barrier, 1, device_id={"mp": ahead(mp, k, n_mp)}, device_id_type=MESH)
 
     for h in range(2):
         loads[h].wait()
 
         @pl.loop(0, half)
         def _(i):
-            if h == 0:
-                pl.semaphore_signal(barrier, 1, device_id={"mp": ahead(mp, i + 1, n_mp)}, device_id_type=MESH)
-            else:
-
-                @pl.when(i > 0)
-                def _():
-                    pl.semaphore_signal(barrier, 1, device_id={"mp": behind(mp, i, n_mp)}, device_id_type=MESH)
-
             at = pl.ds(pl.multiple_of((h * half + i) * shard, 16), shard)
             wide[at, :] = grad_ref[at, :].astype(F32)
 
@@ -108,7 +104,7 @@
             for r in range(counts[q]):
                 dst[s, r] = wide[pl.ds(base + r, half, stride=shard), :].astype(BF16)
 
-    pl.semaphore_wait(barrier, n_dp + n_mp - 2)
+    pl.semaphore_wait(barrier, 2 * (side - 1) + len(NEAR))
 
     def rs1(q, h, f):
         return remote(rs1_out[q].at[h, f], rs1_in[q].at[h, first[h]], rs1_s.at[q, h], rs1_r.at[q, h],
@@ -144,6 +140,8 @@
     for b in range(blocks):
         count = count + jnp.where(owners_ref[b] == mp, 1, 0)
 
+    for k in NEAR:
+        pl.semaphore_signal(near_sem, 1, device_id={"mp": ahead(mp, k, n_mp)}, device_id_type=MESH)
     z32[...] = jnp.zeros_like(z32)
 
     for q in (few, many):
@@ -161,6 +159,8 @@
                         rs2_in[q][h, s, r] = total.astype(BF16)
                 if k < side:
                     rs2(q, h, s).start()
+
+    pl.semaphore_wait(near_sem, len(NEAR))
 
     def z_copy(j, q, src, dst, s, r):
         to = ahead(mp, z_offset(j), n_mp)
@@ -248,9 +248,11 @@
         if i == 0:
             polys = [jnp.where(eye, a0, 0.0) + m for m in mixes]
         else:
-            polys = [a0 * p + dot(p, m) for p, m in zip(polys, mixes)]
+            both = [dot(jnp.concatenate([p, g], axis=0), m) for p, g, m in zip(polys, grams, mixes)]
+            polys = [a0 * p + b[0:128] for p, b in zip(polys, both)]
         if i < ITERS - 1:
-            halves = [a0 * g + dot(m, g) for g, m in zip(grams, mixes)]
+            products = [b[128:] for b in both] if i else [dot(g, m) for g, m in zip(grams, mixes)]
+            halves = [a0 * g + b for g, b in zip(grams, products)]
             grams = [a0 * h + dot(h, m) for h, m in zip(halves, mixes)]
     polys = [p * (-learn_rate * update_gain * math.sqrt(D) / n) for p, n in zip(polys, norms)]
 
@@ -426,6 +428,7 @@
             pltpu.VMEM((2, n_mp, cap * 8, head), BF16),
             pltpu.VMEM((2, n_mp, cap * 8, head), BF16),
             *[pltpu.VMEM((2, SIDE, SIDE, n, half, head), BF16) for n in (few + 1, many)],
+            pltpu.SemaphoreType.REGULAR,
             sem((5,)),
             sem((6,)),
             *[sem((2, 2))] * 4,

time: 96 us -> 93.5 us (0.974)
  the two profiles are of different devices: /device:TPU:32 before, /device:TPU:1 now
where the time goes in v4:
time: 93.5 us; the launch traced here: 91.9 us
  Pallas kernels  91.2 us (98%)
    pallas_call x1, Pallas kernels, body(): pl.pallas_call(functools.partial(kernel, n_dp, n_mp, cap, blocks, rows),...  88.7 us
    pallas_call x1, Pallas kernels, body(): pl.pallas_call(finish, out_shape=(jax.ShapeDtypeStruct((blocks * shard, h...  2.59 us

profile of v4, /device:TPU:1, one launch (start us, length us, event | category | flops | bytes accessed | tf_op | source)
XLA Modules:
  0.0 91.9 jit_solution(12621971615527772109)
XLA Ops:
  0.6 88.7 %muon_step.1 = (bf16[7168,128]{1,0:T(8,128)(2,1)}, f32[1,32]{1,0:T(1,128)}, bf16[2,14,32,128]{3,2,1,0:T(8,128)(2,1)}, f32[2,14,32,128]{3,2,1,0:T(8,128)}) custom-call(s32[32]{0:T(128)} %owners_hbm.1, bf16[7168,128]{1,0:T(8,128)(2,1)} %bitcast.7, bf16[2,14,32,128]{3,2,1,0:T(8,128)(2,1)} %bitcast.9, f32[2,14,32,128]{3,2,1,0:T(8,128)} %bitcast.8), custom_call_target="tpu_custom_call" | custom-call | tf_op jit(solution)/shard_map/muon_step/pallas_call | solution.py:401
  89.3 2.6 %write_results.1 = (bf16[7168,128]{1,0:T(8,128)(2,1)}, f32[1,32]{1,0:T(1,128)}, bf16[2,14,32,128]{3,2,1,0:T(8,128)(2,1)}, f32[2,14,32,128]{3,2,1,0:T(8,128)}) custom-call(bf16[7168,128]{1,0:T(8,128)(2,1)} %get-tuple-element.12.out_in, f32[1,32]{1,0:T(1,128)} %get-tuple-element.13.scale_in, bf16[2,14,32,128]{3,2,1,0:T(8,128)(2,1)} %get-tuple-element.14.newmom_in, ...), custom_call_target="tpu_custom_call" | custom-call | tf_op jit(solution)/shard_map/write_results/pallas_call | solution.py:450

commit v5 on v4

--- a/solution.py
+++ b/solution.py
@@ -144,6 +144,17 @@
         pl.semaphore_signal(near_sem, 1, device_id={"mp": ahead(mp, k, n_mp)}, device_id_type=MESH)
     z32[...] = jnp.zeros_like(z32)
 
+    def z_copy(j, q, src, dst, s, r):
+        to = ahead(mp, z_offset(j), n_mp)
+        return remote(src.at[q, to], dst.at[q, mp], s.at[q], r.at[q], mp=to)
+
+    def z_send(q, src, dst, s, r):
+        @pl.loop(0, n_mp - 1)
+        def _(j):
+            z_copy(j, q, src, dst, s, r).start()
+
+        dst[q, mp] = src[q, mp]
+
     for q in (few, many):
         for h in range(2):
             all_here(rs1_in[q].at[h, 0:side - 1], rs1_r.at[q, h])
@@ -159,21 +170,8 @@
                         rs2_in[q][h, s, r] = total.astype(BF16)
                 if k < side:
                     rs2(q, h, s).start()
-
-    pl.semaphore_wait(near_sem, len(NEAR))
-
-    def z_copy(j, q, src, dst, s, r):
-        to = ahead(mp, z_offset(j), n_mp)
-        return remote(src.at[q, to], dst.at[q, mp], s.at[q], r.at[q], mp=to)
-
-    def z_send(q, src, dst, s, r):
-        @pl.loop(0, n_mp - 1)
-        def _(j):
-            z_copy(j, q, src, dst, s, r).start()
-
-        dst[q, mp] = src[q, mp]
-
-    for q in (few, many):
+        if q == few:
+            pl.semaphore_wait(near_sem, len(NEAR))
         for h in range(2):
             all_here(rs2_in[q].at[h, 0:side - 1], rs2_r.at[q, h])
         for r in range(counts[q]):
@@ -213,8 +211,7 @@
         for d in range(n_dp):
             gram_out[d, c] = gram[d * piece:(d + 1) * piece, :]
 
-    @pl.loop(1, n_dp)
-    def _(k):
+    for k in (10, 9, 11, 6, 14, 5, 7, 13, 15, 2, 8, 1, 3, 4, 12):
         to = ahead(dp, k, n_dp)
         remote(gram_out.at[to], gram_in.at[dp], g_s, g_r, dp=to).start()
 
@@ -227,8 +224,7 @@
         part = part + gram_in[s]
     gram_all[dp] = part
 
-    @pl.loop(1, n_dp)
-    def _(k):
+    for k in (10, 9, 11, 6, 14, 5, 7, 13, 15, 2, 8, 1, 3, 4, 12):
         to = ahead(dp, k, n_dp)
         remote(gram_all.at[dp], gram_all.at[dp], h_s, h_r, dp=to).start()
 
@@ -281,11 +277,11 @@
     stores[1].start()
 
     def ag1(q, h, k, p):
-        return remote(ag[q].at[h, second[h], 0], ag[q].at[h, second[h], k], ag1_s.at[q, h], ag1_r.at[q, h],
+        return remote(ag[q].at[h, second[h], 0], ag[q].at[h, second[h], k], ag1_s.at[q, h, k], ag1_r.at[q, h, k],
                       dp=dp_at(h, p, second[h]))
 
     def ag2(q, h, s, p, part):
-        at = ag[q].at[h, s, 0] if part == 0 else ag[q].at[h, s, pl.ds(1, side - 1)]
+        at = ag[q].at[h, s, part]
         return remote(at, at, ag2_s.at[q, h, part], ag2_r.at[q, h, part], dp=dp_at(h, first[h], p))
 
     sent = (counts[0] + 1, counts[1])
@@ -303,10 +299,12 @@
         for k in range(1, side):
             for h in range(2):
                 ag2(q, h, second[h], ahead(second[h], k, side), 0).start()
-        for h in range(2):
-            all_here(ag[q].at[h, second[h], 1:side], ag1_r.at[q, h])
-            for k in range(1, side):
-                ag2(q, h, second[h], ahead(second[h], k, side), 1).start()
+        for c in (1, 3, 2):
+            for h in range(2):
+                at = ag[q].at[h, second[h], c]
+                remote(at, at, ag1_s.at[q, h, c], ag1_r.at[q, h, c], dp=ahead(dp, 1, n_dp)).wait_recv()
+                for k in (2, 1, 3):
+                    ag2(q, h, second[h], ahead(second[h], k, side), c).start()
 
     def spread(q, h, s, k):
         f = behind(first[h], k, side)
@@ -319,15 +317,12 @@
             for k in range(side):
                 spread(q, h, second[h], k)
     for q in (many, few):
-        for part in range(2):
-            for h in range(2):
-                all_here(ag[q].at[h, 0:side - 1, 0] if part == 0 else ag[q].at[h, 0:side - 1, 1:side], ag2_r.at[q, h, part])
+        for part in (0, 1, 3, 2):
+            for h in range(2):
+                all_here(ag[q].at[h, 0:side - 1, part], ag2_r.at[q, h, part])
                 for k in range(1, side):
                     s = behind(second[h], k, side)
-                    if part == 0:
-                        spread(q, h, s, 0)
-                    else:
-                        pl.loop(1, side)(functools.partial(spread, q, h, s))
+                    spread(q, h, s, part)
 
     both = []
     for h in range(2):
@@ -361,9 +356,10 @@
         for h in range(2):
             all_sent(rs1_out[q].at[h, 0:side - 1], rs1_s.at[q, h])
             all_sent(rs2_out[q].at[h, 0:side - 1], rs2_s.at[q, h])
-            all_sent(ag[q].at[h, 0, 1:side], ag1_s.at[q, h])
-            all_sent(ag[q].at[h, 0:side - 1, 0], ag2_s.at[q, h, 0])
-            all_sent(ag[q].at[h, 0:side - 1, 1:side], ag2_s.at[q, h, 1])
+            for c in range(side):
+                if c:
+                    all_sent(ag[q].at[h, 0, c], ag1_s.at[q, h, c])
+                all_sent(ag[q].at[h, 0:side - 1, c], ag2_s.at[q, h, c])
     all_sent(gram_out.at[0:n_dp - 1], g_s)
     all_sent(gram_all.at[0:n_dp - 1], h_s)
 
@@ -435,8 +431,7 @@
             *[sem((2,))] * 2,
             *[sem(())] * 4,
             *[sem((2,))] * 2,
-            *[sem((2, 2))] * 2,
-            *[sem((2, 2, 2))] * 2,
+            *[sem((2, 2, SIDE))] * 4,
         ],
         compiler_params=pltpu.CompilerParams(
             collective_id=0, has_side_effects=True, vmem_limit_bytes=VMEM),

time: 93.5 us -> 91.4 us (0.978); the launches traced: 91.9 us -> 91.1 us
  no operation moved by 1% of the time
where the time goes in v5:
time: 91.4 us; the launch traced here: 91.1 us
  Pallas kernels  90.5 us (99%)
    pallas_call x1, Pallas kernels, body(): pl.pallas_call(functools.partial(kernel, n_dp, n_mp, cap, blocks, rows),...  87.9 us
    pallas_call x1, Pallas kernels, body(): pl.pallas_call(finish, out_shape=(jax.ShapeDtypeStruct((blocks * shard, h...  2.59 us

profile of v5, /device:TPU:1, one launch (start us, length us, event | category | flops | bytes accessed | tf_op | source)
XLA Modules:
  0.0 91.1 jit_solution(12455693564497321336)
XLA Ops:
  0.6 87.9 %muon_step.1 = (bf16[7168,128]{1,0:T(8,128)(2,1)}, f32[1,32]{1,0:T(1,128)}, bf16[2,14,32,128]{3,2,1,0:T(8,128)(2,1)}, f32[2,14,32,128]{3,2,1,0:T(8,128)}) custom-call(s32[32]{0:T(128)} %owners_hbm.1, bf16[7168,128]{1,0:T(8,128)(2,1)} %bitcast.7, bf16[2,14,32,128]{3,2,1,0:T(8,128)(2,1)} %bitcast.9, f32[2,14,32,128]{3,2,1,0:T(8,128)} %bitcast.8), custom_call_target="tpu_custom_call" | custom-call | tf_op jit(solution)/shard_map/muon_step/pallas_call | solution.py:397
  88.5 2.6 %write_results.1 = (bf16[7168,128]{1,0:T(8,128)(2,1)}, f32[1,32]{1,0:T(1,128)}, bf16[2,14,32,128]{3,2,1,0:T(8,128)(2,1)}, f32[2,14,32,128]{3,2,1,0:T(8,128)}) custom-call(bf16[7168,128]{1,0:T(8,128)(2,1)} %get-tuple-element.12.out_in, f32[1,32]{1,0:T(1,128)} %get-tuple-element.13.scale_in, bf16[2,14,32,128]{3,2,1,0:T(8,128)(2,1)} %get-tuple-element.14.newmom_in, ...), custom_call_target="tpu_custom_call" | custom-call | tf_op jit(solution)/shard_map/write_results/pallas_call | solution.py:445

commit v6 on v5

--- a/solution.py
+++ b/solution.py
@@ -188,6 +188,7 @@
 
     loads[3].wait()
     loads[4].wait()
+    parts_of = [[] for _ in range(cap)]
     for q in (few, many):
         all_here(z_in.at[q, 0:n_mp - 1], z_r.at[q])
         z32[...] = z_in[q].reshape(z32.shape).astype(F32)
@@ -199,15 +200,16 @@
                 after = (decay_rate * before.astype(F32) + arrived).astype(BF16)
                 newmom_ref[c, r] = jnp.where(count > c, after, before)
                 upd[c, pl.ds(r * n_mp, n_mp), :] = arrived + decay_rate * after.astype(F32)
+            u = upd[c, starts[q] * n_mp:(starts[q] + counts[q]) * n_mp, :]
+            parts_of[c].append(lax.dot_general(
+                u, u, (((0,), (0,)), ((), ())), precision=lax.Precision.HIGHEST, preferred_element_type=F32))
 
     stores = [pltpu.make_async_copy(newmom_ref, newmom_hbm, out_sem.at[0])]
     stores[0].start()
 
     piece = 128 // n_dp
     for c in range(cap):
-        u = upd[c]
-        gram = lax.dot_general(u, u, (((0,), (0,)), ((), ())), precision=lax.Precision.HIGHEST,
-                               preferred_element_type=F32)
+        gram = parts_of[c][0] + parts_of[c][1]
         for d in range(n_dp):
             gram_out[d, c] = gram[d * piece:(d + 1) * piece, :]
 

time: 91.4 us -> 91.3 us (level)
  no operation moved by 1% of the time
where the time goes in v6:
time: 91.3 us; the launch traced here: 91 us
  Pallas kernels  90.4 us (99%)
    pallas_call x1, Pallas kernels, body(): pl.pallas_call(functools.partial(kernel, n_dp, n_mp, cap, blocks, rows),...  87.8 us
    pallas_call x1, Pallas kernels, body(): pl.pallas_call(finish, out_shape=(jax.ShapeDtypeStruct((blocks * shard, h...  2.59 us

profile of v6, /device:TPU:1, one launch (start us, length us, event | category | flops | bytes accessed | tf_op | source)
XLA Modules:
  0.0 91.0 jit_solution(12523476312451218226)
XLA Ops:
  0.6 87.8 %muon_step.1 = (bf16[7168,128]{1,0:T(8,128)(2,1)}, f32[1,32]{1,0:T(1,128)}, bf16[2,14,32,128]{3,2,1,0:T(8,128)(2,1)}, f32[2,14,32,128]{3,2,1,0:T(8,128)}) custom-call(s32[32]{0:T(128)} %owners_hbm.1, bf16[7168,128]{1,0:T(8,128)(2,1)} %bitcast.7, bf16[2,14,32,128]{3,2,1,0:T(8,128)(2,1)} %bitcast.9, f32[2,14,32,128]{3,2,1,0:T(8,128)} %bitcast.8), custom_call_target="tpu_custom_call" | custom-call | tf_op jit(solution)/shard_map/muon_step/pallas_call | solution.py:399
  88.4 2.6 %write_results.1 = (bf16[7168,128]{1,0:T(8,128)(2,1)}, f32[1,32]{1,0:T(1,128)}, bf16[2,14,32,128]{3,2,1,0:T(8,128)(2,1)}, f32[2,14,32,128]{3,2,1,0:T(8,128)}) custom-call(bf16[7168,128]{1,0:T(8,128)(2,1)} %get-tuple-element.12.out_in, f32[1,32]{1,0:T(1,128)} %get-tuple-element.13.scale_in, bf16[2,14,32,128]{3,2,1,0:T(8,128)(2,1)} %get-tuple-element.14.newmom_in, ...), custom_call_target="tpu_custom_call" | custom-call | tf_op jit(solution)/shard_map/write_results/pallas_call | solution.py:447
